TPU v7x, 32 devices: a whole 2x2x4 slice. The times are simulated.
32 devices in a mesh: ctx: 8 (over y, x, core), exp: 4 (over z).
Axes of the slice: x: 2, y: 2, z: 4, core: 2. Of those that a mesh axis runs over, the one named last changes fastest.
Arguments:
- hidden_in: bfloat16 [1024, 2880], P('ctx'), may hold values from -6 to 6
- query_input: bfloat16 [1024, 2048], P('ctx', 'exp'), may hold values from -16 to 16
- key_heads_input: bfloat16 [1024, 256], P('ctx'), may hold values from -16 to 16
- value_heads_input: bfloat16 [1024, 256], P('ctx'), may hold values from -6 to 6
- sink_logits: float32 [32], P('exp'), may hold values from 0 to 4
- out_proj: bfloat16 [2048, 2880], P('exp'), may hold values from -0.125 to 0.125
- norm_gain: float32 [2880], replicated, may hold values from 0.5 to 1.5
- expert_ids: int32 [1024, 4], P('ctx'), may hold values from 0 to 7, all different within a row; in each aligned block of 128 rows (0 to 127, 128 to 255, ...) at most 80 rows name the same one
- expert_gates: float32 [1024, 4], P('ctx'), may hold values from 0.1 to 1
- gate_up: bfloat16 [8, 2880, 2, 2880], P('ctx', None, None, 'exp'), may hold values from -0.109375 to 0.109375
- down_proj: bfloat16 [8, 2880, 2880], P('ctx', 'exp'), may hold values from -0.109375 to 0.109375
Outputs:
- layer_out: bfloat16 [1024, 2880], P('ctx', 'exp')
Inputs may be any that keep to these rules, and one draw needn't show every extreme that they name: `expert_ids`: each token names 4 different experts; within the 128 tokens of one device no expert is named by more than 80 tokens.
All inputs are finite; a program needn't handle non-finite values.
Results may differ from a plain program's by a relative error of at most 0.02.
Values may be sent and summed in bfloat16 or wider, within the bound.
A program may use at most 64 MiB of HBM per device.

v0:
```python
import math

import jax
import jax.numpy as jnp
import numpy as np
from jax import lax
from jax.sharding import PartitionSpec as P

D = 2880
QUERY_HEADS = 32
KEY_VALUE_HEADS = 4
HEAD_SIZE = 64


yarn_base = 150000.0
yarn_factor = 32.0
yarn_initial = 4096.0
beta_fast = 32.0
beta_slow = 1.0
neg_large = -1e30


def yarn_frequencies(head_dim):
    half_dim = head_dim // 2

    def correction(rotations):
        return (
            head_dim
            * math.log(yarn_initial / (rotations * 2.0 * math.pi))
            / (2.0 * math.log(yarn_base))
        )

    lower_dim = max(math.floor(correction(beta_fast)), 0)
    upper_dim = min(math.ceil(correction(beta_slow)), head_dim - 1)
    extrap_freq = 1.0 / yarn_base ** (np.arange(0, head_dim, 2) / head_dim)
    interp_freq = extrap_freq / yarn_factor
    ramp_part = np.clip((np.arange(half_dim) - lower_dim) / (upper_dim - lower_dim), 0.0, 1.0)
    extrap_share = 1.0 - ramp_part
    return (interp_freq * (1.0 - extrap_share) + extrap_freq * extrap_share).astype(np.float32)


def rotate_with_yarn(heads_in, token_positions):
    head_dim = heads_in.shape[-1]
    freqs = jnp.asarray(yarn_frequencies(head_dim))
    angles = token_positions.astype(jnp.float32)[:, None] * freqs[None, :]
    factor = 0.1 * math.log(yarn_factor) + 1.0
    cosine = (jnp.cos(angles) * factor)[:, None, :]
    sine = (jnp.sin(angles) * factor)[:, None, :]
    first_half = heads_in[..., : head_dim // 2]
    second_half = heads_in[..., head_dim // 2 :]
    return jnp.concatenate(
        [first_half * cosine - second_half * sine, second_half * cosine + first_half * sine],
        axis=-1,
    )


def route_slots(ids_block, n_experts):
    flat_ids = ids_block.reshape(-1)
    onehot = (flat_ids[:, None] == jnp.arange(n_experts, dtype=jnp.int32)[None, :]).astype(
        jnp.int32
    )
    ranks = jnp.cumsum(onehot, axis=0) - onehot
    return jnp.sum(ranks * onehot, axis=1).reshape(ids_block.shape)


def per_device(
    hidden_in,
    query_input,
    key_heads_input,
    value_heads_input,
    sink_logits,
    out_proj,
    norm_gain,
    expert_ids,
    expert_gates,
    gate_up,
    down_proj,
):
    tok_rows = hidden_in.shape[0]
    ctx_count = lax.axis_size("ctx")
    exp_count = lax.axis_size("exp")
    local_heads = query_input.shape[1] // HEAD_SIZE
    token_positions = lax.axis_index("ctx") * tok_rows + jnp.arange(tok_rows, dtype=jnp.int32)
    q_rot = rotate_with_yarn(
        query_input.astype(jnp.float32).reshape(tok_rows, local_heads, HEAD_SIZE), token_positions
    ).astype(jnp.bfloat16)
    shared_key_head = lax.axis_index("exp") * local_heads // (QUERY_HEADS // KEY_VALUE_HEADS)
    key_block = lax.dynamic_slice_in_dim(key_heads_input, shared_key_head * HEAD_SIZE, HEAD_SIZE, 1)
    value_block = lax.dynamic_slice_in_dim(
        value_heads_input, shared_key_head * HEAD_SIZE, HEAD_SIZE, 1
    )
    key_rot = (
        rotate_with_yarn(
            key_block.astype(jnp.float32).reshape(tok_rows, 1, HEAD_SIZE), token_positions
        )
        .reshape(tok_rows, HEAD_SIZE)
        .astype(jnp.bfloat16)
    )
    key_value = jnp.concatenate([key_rot, value_block], axis=1)
    score_scale = 1.0 / math.sqrt(HEAD_SIZE)
    block_part = lax.all_gather(key_value, "ctx", axis=0, tiled=True)
    run_max = jnp.broadcast_to(sink_logits[:, None], (local_heads, tok_rows))
    run_total = jnp.ones((local_heads, tok_rows), jnp.float32)
    run_sum = jnp.zeros((local_heads, tok_rows, HEAD_SIZE), jnp.float32)
    key_count = block_part.shape[0]
    key_part = block_part[:, :HEAD_SIZE]
    value_part = block_part[:, HEAD_SIZE:].astype(jnp.float32)
    scores = (
        jnp.einsum("rhd,kd->hrk", q_rot, key_part, preferred_element_type=jnp.float32) * score_scale
    )
    key_pos = jnp.arange(key_count, dtype=jnp.int32)
    visible = token_positions[:, None] >= key_pos[None, :]
    scores = jnp.where(visible[None, :, :], scores, neg_large)
    new_max = jnp.maximum(run_max, jnp.max(scores, axis=2))
    weights = jnp.exp(scores - new_max[:, :, None])
    factor = jnp.exp(run_max - new_max)
    run_total = run_total * factor + jnp.sum(weights, axis=2)
    run_sum = run_sum * factor[:, :, None] + jnp.einsum(
        "hrk,kd->hrd", weights, value_part, precision=lax.Precision.HIGHEST
    )
    run_max, run_total, run_sum = (new_max, run_total, run_sum)
    attended = (
        (run_sum / run_total[:, :, None])
        .transpose(1, 0, 2)
        .reshape(tok_rows, local_heads * HEAD_SIZE)
        .astype(jnp.bfloat16)
    )
    head_part = jnp.dot(attended, out_proj, preferred_element_type=jnp.float32)
    residual = hidden_in.astype(jnp.float32) + lax.psum(
        head_part.astype(jnp.bfloat16), "exp"
    ).astype(jnp.float32)
    mean_square = jnp.mean(residual * residual, axis=1, keepdims=True)
    normed = (residual * lax.rsqrt(mean_square + 1e-05) * norm_gain[None, :]).astype(jnp.bfloat16)
    exp_local = gate_up.shape[0]
    n_experts = exp_local * ctx_count
    top_count = expert_ids.shape[1]
    capacity = max(2, tok_rows * top_count * 5 // (4 * n_experts))
    slot_index = route_slots(expert_ids, n_experts)
    dest_row = expert_ids * capacity + slot_index
    spread_rows = jnp.broadcast_to(normed[:, None, :], (tok_rows, top_count, D)).reshape(
        tok_rows * top_count, D
    )
    send_rows = (
        jnp.zeros((n_experts * capacity, D), jnp.bfloat16).at[dest_row.reshape(-1)].set(spread_rows)
    )
    bucket_rows = ctx_count * capacity
    unit_count = gate_up.shape[-1]
    col_width = D // exp_count
    weights_flat = gate_up.reshape(exp_local, D, 2 * unit_count)
    received = lax.all_to_all(
        send_rows.reshape(ctx_count, exp_local * capacity, D),
        "ctx",
        split_axis=0,
        concat_axis=0,
        tiled=True,
    )
    expert_rows = (
        received.reshape(ctx_count, exp_local, capacity, D)
        .transpose(1, 0, 2, 3)
        .reshape(exp_local, bucket_rows, D)
    )
    gate_up_out = jnp.einsum(
        "erd,edf->erf", expert_rows, weights_flat, preferred_element_type=jnp.float32
    )
    gate_up_out = gate_up_out.reshape(exp_local, bucket_rows, 2, unit_count)
    gate_value = gate_up_out[:, :, 0]
    up_value = gate_up_out[:, :, 1]
    activated = ((up_value + 1.0) * gate_value * jax.nn.sigmoid(1.702 * gate_value)).astype(
        jnp.bfloat16
    )
    partial_value = jnp.einsum(
        "erf,efd->erd", activated, down_proj, preferred_element_type=jnp.float32
    )
    partial_rounded = partial_value.astype(jnp.bfloat16)
    outgoing = partial_rounded.reshape(exp_local, ctx_count, capacity, D).transpose(1, 0, 2, 3)
    returned = lax.all_to_all(
        outgoing.reshape(ctx_count, exp_local * capacity, D),
        "ctx",
        split_axis=0,
        concat_axis=0,
        tiled=True,
    )
    picked_rows = returned.reshape(n_experts * capacity, D)[dest_row]
    gated = jnp.sum(expert_gates[:, :, None] * picked_rows.astype(jnp.float32), axis=1)
    moe_cols = lax.psum_scatter(
        gated.astype(jnp.bfloat16), "exp", scatter_dimension=1, tiled=True
    ).astype(jnp.float32)
    residual_cols = lax.dynamic_slice_in_dim(
        residual, lax.axis_index("exp") * col_width, col_width, 1
    )
    return (residual_cols + moe_cols).astype(jnp.bfloat16)


def solution(mesh):
    placed = (
        P("ctx", None),
        P("ctx", "exp"),
        P("ctx", None),
        P("ctx", None),
        P("exp"),
        P("exp", None),
        P(),
        P("ctx", None),
        P("ctx", None),
        P("ctx", None, None, "exp"),
        P("ctx", "exp", None),
    )
    return jax.shard_map(
        per_device, mesh=mesh, in_specs=placed, out_specs=P("ctx", "exp"), check_vma=False
    )
```

profile of v0, /device:TPU:0, one launch (start us, length us, event | category | flops | bytes accessed | tf_op | source)
XLA Modules:
  0.0 270.4 jit_solution(4685126095501453117)
XLA Ops:
  6.5 0.0 copy-start
  6.5 0.0 copy-start.4
  6.5 0.0 all-reduce.2.cloned.1.call-start
  6.6 1.0 constant_dynamic-slice_fusion
  7.6 0.1 copy.62
  7.7 0.8 fusion.39
  8.5 0.8 fusion.33
  9.3 0.1 copy.63
  9.4 10.8 %all_gather.3 = bf16[1024,128]{0,1:T(8,128)(2,1)S(1)} all-gather(bf16[128,128]{0,1:T(8,128)(2,1)S(1)} %pad_maximum_fusion), channel_id=1, replica_groups=mesh['ctx'=8,'exp'=4] {'ctx'}, dimensions={0}, use_global_device_ids=true | all-gather | bytes 294912 | tf_op jit(solution)/shard_map/all_gather | solution.py:101
  20.3 1.0 copy.47
  21.3 0.1 iota_compare_fusion
  21.4 0.7 fusion.5
  22.2 0.0 copy-done.4
  22.2 0.1 broadcast_maximum_fusion
  22.3 0.9 fusion.3
  23.1 0.1 multiply_bitcast_fusion
  23.2 2.4 fusion.21
  25.6 0.0 copy-start.2
  25.6 0.0 copy-done
  25.6 0.0 copy-start.1
  25.7 1.8 convolution_convert_fusion.1
  27.4 0.0 all-reduce.2.cloned.1.call-update
  27.5 0.0 copy-done.2
  27.5 0.1 copy.50
  27.6 0.1 eq.29
  27.7 0.1 eq.25
  27.8 1.3 reduce-window.6
  29.2 0.2 slice_reduce_fusion
  29.4 0.1 fusion.42
  29.5 0.1 reshape.373
  29.6 0.1 copy.52
  29.7 0.1 copy.53
  29.8 0.1 reshape.374
  29.9 40.6 %all-reduce.2.cloned.1.call-done = bf16[128,2880]{0,1:T(8,128)(2,1)} async-done(((bf16[128,2880]{0,1:T(8,128)(2,1)}), bf16[128,2880]{0,1:T(8,128)(2,1)}) %all-reduce.2.cloned.1.call-update) | async-done | bytes 737296 | tf_op jit(solution)/shard_map/psum | solution.py:129
  70.5 2.8 %convert_add_fusion = (f32[128,2880]{0,1:T(8,128)}, f32[128]{0:T(128)S(1)}) fusion(bf16[128,2880]{0,1:T(8,128)(2,1)} %all-reduce.2.cloned.1.call-done, bf16[128,2880]{0,1:T(8,128)(2,1)} %param.13), kind=kLoop, calls=%fused_computation.26 | loop fusion | flops 1843072 | bytes 2949632 | tf_op jit(solution)/shard_map/add | solution.py:129
  73.3 0.0 copy-done.1
  73.3 2.7 multiply_convert_fusion
  76.0 2.3 copy.54
  78.3 3.5 %broadcast_in_dim.27 = bf16[128,4,2880]{2,1,0:T(4,128)(2,1)} broadcast(bf16[128,2880]{1,0:T(8,128)(2,1)} %copy.54), dimensions={0,2} | broadcast | bytes 3686400 | tf_op jit(solution)/shard_map/broadcast_in_dim | solution.py:140
  81.8 5.6 %reshape.397 = bf16[512,2880]{1,0:T(8,128)(2,1)} reshape(bf16[128,4,2880]{2,1,0:T(4,128)(2,1)} %broadcast_in_dim.27) | data formatting | bytes 5898240 | tf_op jit(solution)/shard_map/reshape | solution.py:140
  87.4 8.3 %scatter_custom_fusion = bf16[640,2880]{1,0:T(8,128)(2,1)} fusion(s32[512]{0:T(512)S(1)} %bitcast.84, bf16[512,2880]{1,0:T(8,128)(2,1)} %reshape.397, bf16[]{:T(256)} %constant.65.clone.1), kind=kCustom, calls=%fused_computation.18 | custom fusion | bytes 3686912 | tf_op jit(solution)/shard_map/scatter | solution.py:144
  95.7 0.0 slice-start
  95.7 48.4 %all_to_all.10 = bf16[8,80,2880]{2,1,0:T(8,128)(2,1)S(1)} all-to-all(bf16[8,80,2880]{2,1,0:T(8,128)(2,1)} %bitcast.80), channel_id=1, replica_groups=mesh['ctx'=8,'exp'=4] {'ctx'}, dimensions={0} | all-to-all | bytes 7372800 | tf_op jit(solution)/shard_map/all_to_all | solution.py:150
  144.1 0.0 slice-start.1
  144.1 9.5 %fusion.10 = f32[1,640,2,720]{1,3,2,0:T(8,128)S(1)} fusion(bf16[640,2880,1]{1,0,2:T(8,128)(2,1)S(1)} %bitcast.81, bf16[1,2880,2,720]{1,3,2,0:T(8,128)(2,1)} %param.22), kind=kOutput, calls=%fused_computation.17 | convolution fusion | flops 5308416000 | bytes 15667200 | tf_op jit(solution)/shard_map/erd,edf->erf/dot_general | solution.py:162
  153.6 0.0 slice-done
  153.6 0.0 slice-done.1
  153.7 5.6 %convolution_convert_fusion = bf16[640,2880]{0,1:T(8,128)(2,1)} fusion(bf16[1,720,2880]{2,1,0:T(8,128)(2,1)S(1)} %bitcast.86, f32[1,640,2,720]{1,3,2,0:T(8,128)S(1)} %fusion.10), kind=kOutput, calls=%fused_computation.5 | convolution fusion | flops 2659737600 | bytes 11520000 | tf_op jit(solution)/shard_map/erf,efd->erd/dot_general | solution.py:171
  159.2 6.2 %copy.56 = bf16[640,2880]{1,0:T(8,128)(2,1)} copy(bf16[640,2880]{0,1:T(8,128)(2,1)} %convolution_convert_fusion) | data formatting | bytes 7372800 | tf_op jit(solution)/shard_map/convert_element_type | solution.py:174
  165.4 0.0 copy-start.3
  165.4 4.6 %all-to-all-start.1 = ((bf16[8,80,2880]{2,1,0:T(8,128)(2,1)}), bf16[8,80,2880]{2,1,0:T(8,128)(2,1)}, u32[]{:S(2)}, u32[]{:S(2)}) async-start(bf16[8,80,2880]{2,1,0:T(8,128)(2,1)} %bitcast.79), calls=%async_computation.1 | async-start | bytes 7536640 | tf_op jit(solution)/shard_map/all_to_all | solution.py:176
  170.0 0.0 reduce-scatter.2.cloned.1.call-start
  170.1 0.1 copy.57
  170.2 0.1 reshape.387
  170.3 0.0 copy-done.3
  170.3 0.1 copy.49
  170.4 44.2 %all-to-all-done.1 = bf16[8,80,2880]{2,1,0:T(8,128)(2,1)} async-done(((bf16[8,80,2880]{2,1,0:T(8,128)(2,1)}), bf16[8,80,2880]{2,1,0:T(8,128)(2,1)}, u32[]{:S(2)}, u32[]{:S(2)}) %all-to-all-start.1) | async-done | bytes 3686432 | tf_op jit(solution)/shard_map/all_to_all | solution.py:176
  214.6 9.7 %gather_fusion = bf16[512,2880]{1,0:T(8,128)(2,1)} fusion(bf16[640,2880]{1,0:T(8,128)(2,1)} %bitcast.24, s32[1024]{0:T(1024)S(1)} %pad_clamp_fusion), kind=kCustom, calls=%fused_computation | custom fusion | bytes 5900288 | tf_op jit(solution)/shard_map/gather | solution.py:183
  224.2 6.5 %reshape.403 = f32[128,4,2880]{2,1,0:T(4,128)} reshape(bf16[512,2880]{1,0:T(8,128)(2,1)} %gather_fusion) | data formatting | bytes 8847360 | tf_op jit(solution)/shard_map/convert_element_type | solution.py:184
  230.8 7.9 %multiply_reduce_fusion = bf16[128,2880]{1,0:T(8,128)(2,1)} fusion(f32[128,4,2880]{2,1,0:T(4,128)} %reshape.403, f32[128,4]{1,0:T(8,128)S(1)} %copy.49), kind=kLoop, calls=%fused_computation.4 | loop fusion | flops 2580480 | bytes 6637568 | tf_op jit(solution)/shard_map/reduce_sum | solution.py:184
  238.7 2.3 copy.58
  241.0 0.0 reduce-scatter.2.cloned.1.call-update
  241.0 20.8 %reduce-scatter.2.cloned.1.call-done = bf16[128,720]{0,1:T(8,128)(2,1)} async-done(((bf16[128,2880]{0,1:T(8,128)(2,1)}), bf16[128,720]{0,1:T(8,128)(2,1)}) %reduce-scatter.2.cloned.1.call-update) | async-done | bytes 184336 | tf_op jit(solution)/shard_map/reduce_scatter | solution.py:185
  261.8 1.8 add_convert_fusion
  (14 shorter events, 0.1 us)
Async XLA Ops:
  6.5 19.1 %copy-start = (bf16[512,2880]{0,1:T(8,128)(2,1)S(1)}, bf16[512,2880]{0,1:T(8,128)(2,1)}, u32[]{:S(2)}) copy-start(bf16[512,2880]{0,1:T(8,128)(2,1)} %param.18) | copy-start | bytes 8847364
  6.5 15.6 %copy-start.4 = (f32[8]{0:T(128)S(1)}, f32[8]{0:T(128)}, u32[]{:S(2)}) copy-start(f32[8]{0:T(128)} %param.17) | copy-start | bytes 100
  6.5 64.0 %all-reduce.2.cloned.1.call-start = ((), (), s32[]{:S(2)}) async-start(), calls=%async_computation.3 | async-start | bytes 1474560 | tf_op jit(solution)/shard_map/psum | solution.py:129
  25.6 1.9 copy-start.2
  25.6 47.7 %copy-start.1 = (f32[2880]{0:T(1024)S(1)}, f32[2880]{0:T(1024)}, u32[]{:S(2)}) copy-start(f32[2880]{0:T(1024)} %param.19) | copy-start | bytes 34564
  95.7 57.9 %slice-start = ((s8[4239360]{0:T(1024)(128)(4,1)}), s8[4194304]{0:T(1024)(128)(4,1)S(1)}, s32[]{:S(2)}) async-start(s8[4239360]{0:T(1024)(128)(4,1)} %bitcast.85), calls=%async_computation.5 | async-start | bytes 8388608
  144.1 9.5 %slice-start.1 = ((s8[4239360]{0:T(1024)(128)(4,1)}), s8[45056]{0:T(1024)(128)(4,1)S(1)}, s32[]{:S(2)}) async-start(s8[4239360]{0:T(1024)(128)(4,1)} %bitcast.85), calls=%async_computation.6 | async-start | bytes 90112
  165.4 4.9 %copy-start.3 = (f32[128,4]{0,1:T(4,128)S(1)}, f32[128,4]{0,1:T(4,128)}, u32[]{:S(2)}) copy-start(f32[128,4]{0,1:T(4,128)} %param.21) | copy-start | bytes 6148
  165.4 49.2 %all-to-all-start.1 = ((bf16[8,80,2880]{2,1,0:T(8,128)(2,1)}), bf16[8,80,2880]{2,1,0:T(8,128)(2,1)}, u32[]{:S(2)}, u32[]{:S(2)}) async-start(bf16[8,80,2880]{2,1,0:T(8,128)(2,1)} %bitcast.79), calls=%async_computation.1 | async-start | bytes 7536640 | tf_op jit(solution)/shard_map/all_to_all | solution.py:176
  170.0 91.8 %reduce-scatter.2.cloned.1.call-start = ((), (), s32[]{:S(2)}) async-start(), calls=%async_computation.4 | async-start | bytes 921600 | tf_op jit(solution)/shard_map/reduce_scatter | solution.py:185
Sparse Core Ops, SparseCore 0:
  27.6 42.8 all-reduce.1
  241.1 20.5 reduce-scatter.1
where the time goes:
time: 271 us; the launch traced here: 270 us
  waiting for transfers between devices  106 us (39%)
  blocking collectives  59.2 us (22%)
  local copies, waits for them, and re-layouts  47.8 us (18%)
  matrix products  20 us (7%)
  other arithmetic  19.5 us (7%)
  between operations  13.7 us (5%)
  starting transfers between devices  4.68 us (2%)
    all_to_all x1, blocking collectives, per_device(): lax.all_to_all(send_rows.reshape(ctx_count, exp_local * capacity, D), 'ct...  48.4 us
    all_to_all x1, waiting for transfers between devices, per_device(): lax.all_to_all(outgoing.reshape(ctx_count, exp_local * capacity, D), 'ctx...  44.2 us
    psum x1, waiting for transfers between devices, per_device(): lax.psum(head_part.astype(jnp.bfloat16), 'exp').astype(jnp.float32)  40.6 us
    reduce_scatter x1, waiting for transfers between devices, per_device(): lax.psum_scatter(gated.astype(jnp.bfloat16), 'exp', scatter_dimension=1,...  20.8 us
    all_gather x1, blocking collectives, per_device(): block_part = lax.all_gather(key_value, 'ctx', axis=0, tiled=True)  10.8 us
    gather x1, local copies, waits for them, and re-layouts, per_device(): picked_rows = returned.reshape(n_experts * capacity, D)[dest_row]  9.65 us
    dot_general x1, matrix products, per_device(): jnp.einsum('erd,edf->erf', expert_rows, weights_flat, preferred_element_t...  9.5 us
    scatter x1, local copies, waits for them, and re-layouts, per_device(): jnp.zeros((n_experts * capacity, D), jnp.bfloat16).at[dest_row.reshape(-1)]  8.31 us
  transfers between devices with their start and end apart: 3, of which 3 were waited for; matrix products, arithmetic and copies ran while one was open for 1% of the time, Pallas kernels for 0%

commit v1 on v0

--- a/solution.py
+++ b/solution.py
@@ -54,13 +54,17 @@
     )
 
 
-def route_slots(ids_block, n_experts):
-    flat_ids = ids_block.reshape(-1)
-    onehot = (flat_ids[:, None] == jnp.arange(n_experts, dtype=jnp.int32)[None, :]).astype(
-        jnp.int32
-    )
-    ranks = jnp.cumsum(onehot, axis=0) - onehot
-    return jnp.sum(ranks * onehot, axis=1).reshape(ids_block.shape)
+def routing_matrices(all_ids, all_gates, blocks, rows, capacity):
+    mine = all_ids == lax.axis_index("ctx").astype(jnp.float32)
+    chosen = jnp.sum(mine.astype(jnp.float32), axis=1).reshape(blocks, rows)
+    gate = jnp.sum(jnp.where(mine, all_gates, 0.0), axis=1).reshape(blocks, rows)
+    earlier = jnp.triu(jnp.ones((rows, rows), jnp.bfloat16), 1)
+    slot = jnp.dot(chosen.astype(jnp.bfloat16), earlier, preferred_element_type=jnp.float32)
+    place = jnp.arange(capacity, dtype=jnp.float32)[None, :, None]
+    hit = (slot[:, None, :] == place) & (chosen[:, None, :] > 0.0)
+    pick = hit.astype(jnp.bfloat16)
+    weighted = jnp.where(hit, gate[:, None, :], 0.0).astype(jnp.bfloat16)
+    return pick, weighted
 
 
 def per_device(
@@ -96,15 +100,22 @@
         .reshape(tok_rows, HEAD_SIZE)
         .astype(jnp.bfloat16)
     )
-    key_value = jnp.concatenate([key_rot, value_block], axis=1)
+    ids_part = expert_ids.astype(jnp.bfloat16)
+    gate_high = expert_gates.astype(jnp.bfloat16)
+    gate_low = (expert_gates - gate_high.astype(jnp.float32)).astype(jnp.bfloat16)
+    top_count = expert_ids.shape[1]
+    key_value = jnp.concatenate([key_rot, value_block, ids_part, gate_high, gate_low], axis=1)
     score_scale = 1.0 / math.sqrt(HEAD_SIZE)
     block_part = lax.all_gather(key_value, "ctx", axis=0, tiled=True)
+    routing = block_part[:, 2 * HEAD_SIZE :].astype(jnp.float32)
+    all_ids = routing[:, :top_count]
+    all_gates = routing[:, top_count : 2 * top_count] + routing[:, 2 * top_count :]
     run_max = jnp.broadcast_to(sink_logits[:, None], (local_heads, tok_rows))
     run_total = jnp.ones((local_heads, tok_rows), jnp.float32)
     run_sum = jnp.zeros((local_heads, tok_rows, HEAD_SIZE), jnp.float32)
     key_count = block_part.shape[0]
     key_part = block_part[:, :HEAD_SIZE]
-    value_part = block_part[:, HEAD_SIZE:].astype(jnp.float32)
+    value_part = block_part[:, HEAD_SIZE : 2 * HEAD_SIZE].astype(jnp.float32)
     scores = (
         jnp.einsum("rhd,kd->hrk", q_rot, key_part, preferred_element_type=jnp.float32) * score_scale
     )
@@ -126,69 +137,53 @@
         .astype(jnp.bfloat16)
     )
     head_part = jnp.dot(attended, out_proj, preferred_element_type=jnp.float32)
-    residual = hidden_in.astype(jnp.float32) + lax.psum(
-        head_part.astype(jnp.bfloat16), "exp"
+    share_rows = tok_rows // exp_count
+    my_row = lax.axis_index("exp") * share_rows
+    residual = lax.dynamic_slice_in_dim(hidden_in, my_row, share_rows, 0).astype(
+        jnp.float32
+    ) + lax.psum_scatter(
+        head_part.astype(jnp.bfloat16), "exp", scatter_dimension=0, tiled=True
     ).astype(jnp.float32)
     mean_square = jnp.mean(residual * residual, axis=1, keepdims=True)
     normed = (residual * lax.rsqrt(mean_square + 1e-05) * norm_gain[None, :]).astype(jnp.bfloat16)
-    exp_local = gate_up.shape[0]
-    n_experts = exp_local * ctx_count
-    top_count = expert_ids.shape[1]
+    all_normed = lax.all_gather(normed, ("ctx", "exp"), axis=0, tiled=True)
+    n_experts = gate_up.shape[0] * ctx_count
     capacity = max(2, tok_rows * top_count * 5 // (4 * n_experts))
-    slot_index = route_slots(expert_ids, n_experts)
-    dest_row = expert_ids * capacity + slot_index
-    spread_rows = jnp.broadcast_to(normed[:, None, :], (tok_rows, top_count, D)).reshape(
-        tok_rows * top_count, D
-    )
-    send_rows = (
-        jnp.zeros((n_experts * capacity, D), jnp.bfloat16).at[dest_row.reshape(-1)].set(spread_rows)
-    )
-    bucket_rows = ctx_count * capacity
+    pick, weighted = routing_matrices(all_ids, all_gates, ctx_count, tok_rows, capacity)
+    expert_rows = jnp.einsum(
+        "bst,btd->bsd",
+        pick,
+        all_normed.reshape(ctx_count, tok_rows, D),
+        preferred_element_type=jnp.float32,
+    ).astype(jnp.bfloat16)
+    expert_rows = expert_rows.reshape(ctx_count * capacity, D)
     unit_count = gate_up.shape[-1]
-    col_width = D // exp_count
-    weights_flat = gate_up.reshape(exp_local, D, 2 * unit_count)
-    received = lax.all_to_all(
-        send_rows.reshape(ctx_count, exp_local * capacity, D),
-        "ctx",
-        split_axis=0,
-        concat_axis=0,
-        tiled=True,
-    )
-    expert_rows = (
-        received.reshape(ctx_count, exp_local, capacity, D)
-        .transpose(1, 0, 2, 3)
-        .reshape(exp_local, bucket_rows, D)
-    )
-    gate_up_out = jnp.einsum(
-        "erd,edf->erf", expert_rows, weights_flat, preferred_element_type=jnp.float32
-    )
-    gate_up_out = gate_up_out.reshape(exp_local, bucket_rows, 2, unit_count)
-    gate_value = gate_up_out[:, :, 0]
-    up_value = gate_up_out[:, :, 1]
+    gate_up_out = jnp.dot(
+        expert_rows, gate_up.reshape(D, 2 * unit_count), preferred_element_type=jnp.float32
+    )
+    gate_value = gate_up_out[:, :unit_count]
+    up_value = gate_up_out[:, unit_count:]
     activated = ((up_value + 1.0) * gate_value * jax.nn.sigmoid(1.702 * gate_value)).astype(
         jnp.bfloat16
     )
-    partial_value = jnp.einsum(
-        "erf,efd->erd", activated, down_proj, preferred_element_type=jnp.float32
-    )
-    partial_rounded = partial_value.astype(jnp.bfloat16)
-    outgoing = partial_rounded.reshape(exp_local, ctx_count, capacity, D).transpose(1, 0, 2, 3)
-    returned = lax.all_to_all(
-        outgoing.reshape(ctx_count, exp_local * capacity, D),
-        "ctx",
-        split_axis=0,
-        concat_axis=0,
-        tiled=True,
-    )
-    picked_rows = returned.reshape(n_experts * capacity, D)[dest_row]
-    gated = jnp.sum(expert_gates[:, :, None] * picked_rows.astype(jnp.float32), axis=1)
-    moe_cols = lax.psum_scatter(
-        gated.astype(jnp.bfloat16), "exp", scatter_dimension=1, tiled=True
+    partial_value = jnp.dot(
+        activated, down_proj.reshape(unit_count, D), preferred_element_type=jnp.float32
+    ).astype(jnp.bfloat16)
+    spread = jnp.einsum(
+        "bst,bsd->btd",
+        weighted,
+        partial_value.reshape(ctx_count, capacity, D),
+        preferred_element_type=jnp.float32,
+    ).astype(jnp.bfloat16)
+    gated = lax.psum_scatter(
+        spread.reshape(ctx_count * tok_rows, D), "ctx", scatter_dimension=0, tiled=True
     ).astype(jnp.float32)
-    residual_cols = lax.dynamic_slice_in_dim(
-        residual, lax.axis_index("exp") * col_width, col_width, 1
-    )
-    return (residual_cols + moe_cols).astype(jnp.bfloat16)
+    total = gated + lax.dynamic_update_slice_in_dim(
+        jnp.zeros((tok_rows, D), jnp.float32), residual, my_row, 0
+    )
+    return lax.psum_scatter(
+        total.astype(jnp.bfloat16), "exp", scatter_dimension=1, tiled=True
+    )
 
 
 def solution(mesh):

time: 271 us -> 261 us (0.963)
  waiting for transfers between devices: 106 us -> 169 us
  blocking collectives: 59.2 us -> 12 us
  local copies, waits for them, and re-layouts: 47.8 us -> 22.7 us
  matrix products: 20 us -> 32.7 us
  other arithmetic: 19.5 us -> 10.3 us
  starting transfers between devices: 4.68 us -> 0.31 us
    all_gather x0 -> x1, waiting for transfers between devices: none -> 66.3 us  [per_device(): all_normed = lax.all_gather(normed, ('ctx', 'exp'), axis=0, tiled=True)]
    reduce_scatter x1 -> x2, waiting for transfers between devices: 20.8 us -> 79.1 us  [the longest x1 59.4 us: per_device(): lax.psum_scatter(spread.reshape(ctx_count * tok_rows, D), 'ctx', scatter_...]
    all_to_all x1 -> x0, blocking collectives: 48.4 us -> none  [per_device(): lax.all_to_all(send_rows.reshape(ctx_count, exp_local * capacity, D), 'ct...]
    all_to_all x1 -> x0, waiting for transfers between devices: 44.2 us -> none  [per_device(): lax.all_to_all(outgoing.reshape(ctx_count, exp_local * capacity, D), 'ctx...]
    psum x1 -> x0, waiting for transfers between devices: 40.6 us -> none  [per_device(): lax.psum(head_part.astype(jnp.bfloat16), 'exp').astype(jnp.float32)]
    unnamed x2 -> x5, waiting for transfers between devices: 0.03 us -> 23.1 us
    dot_general x2 -> x5, matrix products: 15.1 us -> 25.8 us  [the longest x1 9.47 us: per_device(): jnp.dot(expert_rows, gate_up.reshape(D, 2 * unit_count), preferred_elemen...]
    gather x1 -> x0, local copies, waits for them, and re-layouts: 9.65 us -> none  [per_device(): picked_rows = returned.reshape(n_experts * capacity, D)[dest_row]]
  transfers between devices with their start and end apart: 3 -> 4, of which waited for: 3 -> 4; matrix products, arithmetic and copies ran while one was open for 1% -> 2% of each run, Pallas kernels for 0% -> 0%
where the time goes in v1:
time: 261 us; the launch traced here: 260 us
  waiting for transfers between devices  169 us (65%)
  matrix products  32.7 us (13%)
  local copies, waits for them, and re-layouts  22.7 us (9%)
  between operations  13.4 us (5%)
  blocking collectives  12 us (5%)
  other arithmetic  10.3 us (4%)
    all_gather x1, waiting for transfers between devices, per_device(): all_normed = lax.all_gather(normed, ('ctx', 'exp'), axis=0, tiled=True)  66.3 us
    reduce_scatter x1, waiting for transfers between devices, per_device(): lax.psum_scatter(spread.reshape(ctx_count * tok_rows, D), 'ctx', scatter_...  59.4 us
    unnamed x5, waiting for transfers between devices  23.1 us
    reduce_scatter x1, waiting for transfers between devices, per_device(): lax.psum_scatter(head_part.astype(jnp.bfloat16), 'exp', scatter_dimension...  19.7 us
    all_gather x1, blocking collectives, per_device(): block_part = lax.all_gather(key_value, 'ctx', axis=0, tiled=True)  12 us
    dot_general x1, matrix products, per_device(): jnp.dot(expert_rows, gate_up.reshape(D, 2 * unit_count), preferred_elemen...  9.47 us
    convert_element_type x1, local copies, waits for them, and re-layouts, per_device(): spread = jnp.einsum('bst,bsd->btd', weighted, partial_value.reshape(ctx_c...  8.43 us
    dot_general x1, matrix products, per_device(): jnp.einsum('bst,bsd->btd', weighted, partial_value.reshape(ctx_count, cap...  6.57 us
  transfers between devices with their start and end apart: 4, of which 4 were waited for; matrix products, arithmetic and copies ran while one was open for 2% of the time, Pallas kernels for 0%

profile of v1, /device:TPU:0, one launch (start us, length us, event | category | flops | bytes accessed | tf_op | source)
XLA Modules:
  0.0 259.9 jit_solution(6154521941079451836)
XLA Ops:
  6.5 0.0 copy-start
  6.5 0.0 copy-start.3
  6.5 0.0 reduce-scatter.6.cloned.1.call-start
  6.6 0.8 convert_element_type.87
  7.4 0.8 subtract_convert_fusion.1
  8.2 0.9 constant_dynamic-slice_fusion.1
  9.0 0.1 copy.46
  9.1 0.1 copy.45
  9.3 0.8 fusion.43
  10.1 0.8 fusion.37
  10.9 0.1 iota_compare_fusion
  11.0 0.1 concatenate.12
  11.0 12.0 %all_gather.6 = bf16[1024,140]{0,1:T(8,128)(2,1)} all-gather(bf16[128,140]{0,1:T(8,128)(2,1)S(1)} %concatenate.12), channel_id=1, replica_groups=mesh['ctx'=8,'exp'=4] {'ctx'}, dimensions={0}, use_global_device_ids=true | all-gather | bytes 322560 | tf_op jit(solution)/shard_map/all_gather | solution.py:109
  23.0 1.0 copy.35
  24.1 1.6 fusion.3
  25.7 0.0 copy-done.3
  25.8 0.1 broadcast_maximum_fusion
  25.8 0.9 fusion.1
  26.7 0.1 multiply_bitcast_fusion
  26.8 3.3 %fusion.14 = bf16[128,8,64]{0,2,1:T(8,128)(2,1)S(1)} fusion(f32[1024,128,8]{1,0,2:T(8,128)S(1)} %get-tuple-element.18, f32[8,128]{1,0:T(8,128)S(1)} %broadcast_maximum_fusion, pred[128,1024]{0,1:T(8,128)(4,1)S(1)} %iota_compare_fusion, bf16[1024,140]{0,1:T(8,128)(2,1)} %all_gather.6, f32[128,8]{0,1:T(8,128)S(1)} %get-tuple-element.14, ...), kind=kOutput, calls=%fused_computation.21 | convolution fusion | flops 808648704 | bytes 4599808 | tf_op jit(solution)/shard_map/hrk,kd->hrd/dot_general | solution.py:129
  30.1 0.0 copy-start.2
  30.1 0.0 copy-done
  30.1 2.0 convolution_convert_fusion.3
  32.1 0.0 reduce-scatter.6.cloned.1.call-update
  32.1 0.0 all-gather.2.cloned.1.call-start
  32.2 2.3 constant_dynamic-slice_fusion
  34.5 1.4 copy.47
  35.8 19.7 %reduce-scatter.6.cloned.1.call-done = bf16[32,2880]{1,0:T(8,128)(2,1)} async-done(((bf16[128,2880]{1,0:T(8,128)(2,1)}), bf16[32,2880]{1,0:T(8,128)(2,1)}) %reduce-scatter.6.cloned.1.call-update) | async-done | bytes 184336 | tf_op jit(solution)/shard_map/reduce_scatter | solution.py:144
  55.6 1.1 multiply_reduce_fusion
  56.7 0.0 copy-done.2
  56.7 1.7 multiply_convert_fusion
  58.4 0.0 all-gather.2.cloned.1.call-update
  58.4 0.2 reduce-scatter.8.cloned.1.call-start
  58.7 0.8 slice_convert_fusion
  59.5 0.1 fusion.31
  59.6 66.3 %all-gather.2.cloned.1.call-done = bf16[1024,2880]{1,0:T(8,128)(2,1)} async-done(((bf16[32,2880]{1,0:T(8,128)(2,1)}), bf16[1024,2880]{1,0:T(8,128)(2,1)}) %all-gather.2.cloned.1.call-update) | async-done | bytes 5898256 | tf_op jit(solution)/shard_map/all_gather | solution.py:149
  125.9 0.0 slice-start
  125.9 4.0 %convolution_convert_fusion.2 = bf16[8,80,2880]{2,1,0:T(8,128)(2,1)S(1)} fusion(bf16[8,128,2880]{2,1,0:T(8,128)(2,1)} %bitcast.67, f32[8,128]{1,0:T(8,128)S(1)} %fusion.31, pred[8,128]{1,0:T(8,128)(4,1)S(1)} %compare_bitcast_fusion), kind=kOutput, calls=%fused_computation.2 | convolution fusion | flops 473866240 | bytes 9589760 | tf_op jit(solution)/shard_map/bst,btd->bsd/dot_general | solution.py:153
  129.9 0.0 slice-start.1
  130.0 9.5 %fusion.60 = f32[640,1440]{0,1:T(8,128)S(1)} fusion(bf16[640,2880]{1,0:T(8,128)(2,1)S(1)} %bitcast.69, bf16[2880,1440]{0,1:T(8,128)(2,1)} %bitcast.74), kind=kOutput, calls=%fused_computation.97 | convolution fusion | flops 5308416000 | bytes 15667200 | tf_op jit(solution)/shard_map/dot_general | solution.py:161
  139.4 0.0 slice-done
  139.4 0.0 slice-done.1
  139.5 5.6 %convolution_convert_fusion.1 = bf16[640,2880]{0,1:T(8,128)(2,1)} fusion(bf16[1,720,2880]{2,1,0:T(8,128)(2,1)S(1)} %bitcast.76, f32[640,1440]{0,1:T(8,128)S(1)} %fusion.60), kind=kOutput, calls=%fused_computation.1 | convolution fusion | flops 2659737600 | bytes 11520000 | tf_op jit(solution)/shard_map/dot_general | solution.py:169
  145.0 6.2 %copy.38 = bf16[640,2880]{1,0:T(8,128)(2,1)} copy(bf16[640,2880]{0,1:T(8,128)(2,1)} %convolution_convert_fusion.1) | data formatting | bytes 7372800 | tf_op jit(solution)/shard_map/convert_element_type | solution.py:171
  151.2 6.6 %convolution_convert_fusion = bf16[8,128,2880]{1,2,0:T(8,128)(2,1)} fusion(bf16[8,80,2880]{2,1,0:T(8,128)(2,1)} %bitcast.68, bf16[8,128]{1,0:T(8,128)(2,1)S(1)} %bitcast.73, f32[8,128]{1,0:T(8,128)S(1)} %fusion.31, pred[8,128]{1,0:T(8,128)(4,1)S(1)} %compare_bitcast_fusion), kind=kOutput, calls=%fused_computation | convolution fusion | flops 475054080 | bytes 9591808 | tf_op jit(solution)/shard_map/bst,bsd->btd/dot_general | solution.py:172
  157.8 8.4 %copy.39 = bf16[8,128,2880]{2,1,0:T(8,128)(2,1)} copy(bf16[8,128,2880]{1,2,0:T(8,128)(2,1)} %convolution_convert_fusion) | data formatting | bytes 11796480 | tf_op jit(solution)/shard_map/convert_element_type | solution.py:177
  166.2 0.0 copy-start.1
  166.2 0.0 reduce-scatter.8.cloned.1.call-update
  166.2 0.0 reduce-scatter.10.cloned.1.call-start
  166.3 59.4 %reduce-scatter.8.cloned.1.call-done = bf16[128,2880]{1,0:T(8,128)(2,1)} async-done(((bf16[1024,2880]{1,0:T(8,128)(2,1)}), bf16[128,2880]{1,0:T(8,128)(2,1)}) %reduce-scatter.8.cloned.1.call-update) | async-done | bytes 737296 | tf_op jit(solution)/shard_map/reduce_scatter | solution.py:178
  225.7 1.2 convert_element_type.107
  226.9 0.0 copy-done.1
  227.0 0.1 add_dynamic-update-slice_fusion
  227.0 1.0 convert_element_type.109
  228.0 2.3 copy.43
  230.3 0.0 reduce-scatter.10.cloned.1.call-update
  230.3 23.0 %reduce-scatter.10.cloned.1.call-done = bf16[720,128]{1,0:T(8,128)(2,1)} async-done(((bf16[2880,128]{1,0:T(8,128)(2,1)}), bf16[720,128]{1,0:T(8,128)(2,1)}) %reduce-scatter.10.cloned.1.call-update) | async-done | bytes 184336
  (9 shorter events, 0.1 us)
Async XLA Ops:
  6.5 23.6 %copy-start = (bf16[512,2880]{0,1:T(8,128)(2,1)S(1)}, bf16[512,2880]{0,1:T(8,128)(2,1)}, u32[]{:S(2)}) copy-start(bf16[512,2880]{0,1:T(8,128)(2,1)} %param.18) | copy-start | bytes 8847364
  6.5 19.2 %copy-start.3 = (f32[8]{0:T(128)S(1)}, f32[8]{0:T(128)}, u32[]{:S(2)}) copy-start(f32[8]{0:T(128)} %param.17) | copy-start | bytes 100
  6.5 49.0 %reduce-scatter.6.cloned.1.call-start = ((), (), s32[]{:S(2)}) async-start(), calls=%async_computation.3 | async-start | bytes 942080 | tf_op jit(solution)/shard_map/reduce_scatter | solution.py:144
  30.1 26.6 %copy-start.2 = (f32[2880]{0:T(1024)S(1)}, f32[2880]{0:T(1024)}, u32[]{:S(2)}) copy-start(f32[2880]{0:T(1024)} %param.19) | copy-start | bytes 34564
  32.1 93.8 %all-gather.2.cloned.1.call-start = ((), (), s32[]{:S(2)}) async-start(), calls=%async_computation.4 | async-start | bytes 6217728 | tf_op jit(solution)/shard_map/all_gather | solution.py:149
  58.4 167.3 %reduce-scatter.8.cloned.1.call-start = ((), (), s32[]{:S(2)}) async-start(), calls=%async_computation.5 | async-start | bytes 6782976 | tf_op jit(solution)/shard_map/reduce_scatter | solution.py:178
  125.9 13.5 %slice-start = ((s8[4239360]{0:T(1024)(128)(4,1)}), s8[4194304]{0:T(1024)(128)(4,1)S(1)}, s32[]{:S(2)}) async-start(s8[4239360]{0:T(1024)(128)(4,1)} %bitcast.75), calls=%async_computation.7 | async-start | bytes 8388608
  129.9 9.5 %slice-start.1 = ((s8[4239360]{0:T(1024)(128)(4,1)}), s8[45056]{0:T(1024)(128)(4,1)S(1)}, s32[]{:S(2)}) async-start(s8[4239360]{0:T(1024)(128)(4,1)} %bitcast.75), calls=%async_computation.8 | async-start | bytes 90112
  166.2 60.7 %copy-start.1 = (bf16[32,2880]{1,0:T(8,128)(2,1)S(1)}, bf16[32,2880]{1,0:T(8,128)(2,1)}, u32[]{:S(2)}) copy-start(bf16[32,2880]{1,0:T(8,128)(2,1)} %reduce-scatter.6.cloned.1.call-done) | copy-start | bytes 552964
  166.2 87.1 %reduce-scatter.10.cloned.1.call-start = ((), (), s32[]{:S(2)}) async-start(), calls=%async_computation.6 | async-start | bytes 921600
Sparse Core Ops, SparseCore 0:
  32.3 23.2 reduce-scatter.5
  58.5 67.3 all-gather.1
  166.4 59.3 reduce-scatter.7
  230.4 22.8 reduce-scatter.9

commit v2 on v1

--- a/solution.py
+++ b/solution.py
@@ -4,6 +4,8 @@
 import jax.numpy as jnp
 import numpy as np
 from jax import lax
+from jax.experimental import pallas as pl
+from jax.experimental.pallas import tpu as pltpu
 from jax.sharding import PartitionSpec as P
 
 D = 2880
@@ -65,6 +67,283 @@
     pick = hit.astype(jnp.bfloat16)
     weighted = jnp.where(hit, gate[:, None, :], 0.0).astype(jnp.bfloat16)
     return pick, weighted
+
+
+PLANE_CTX = 8
+PLANE_EXP = 4
+
+
+def layer_kernel(
+    head_ref, hidden_ref, gain_ref, pick_ref, spread_ref, gu_hbm, down_hbm, out_ref,
+    gu, down, zin, residual, normed, rows, moe, core_in, first_in, second_in, total, stage, zout,
+    send_sems, recv_sems, load_sems,
+):
+    c, e = lax.axis_index("ctx"), lax.axis_index("exp")
+    y, x, k = c // 4, c // 2 % 2, c % 2
+    blk = head_ref.shape[0]
+    share = blk // PLANE_EXP
+    half = blk // 2
+    cap = pick_ref.shape[1]
+    col = out_ref.shape[1]
+
+    def at(pos, core):
+        return (y + pos // 2) % 2 * 4 + (x + pos % 2) % 2 * 2 + core
+
+    mate = at(0, 1 - k)
+    ids = {}
+
+    def copy(name, src, dst, ctx, exp):
+        sem = ids.setdefault(name, len(ids))
+        return pltpu.make_async_remote_copy(
+            src_ref=src,
+            dst_ref=dst,
+            send_sem=send_sems.at[sem],
+            recv_sem=recv_sems.at[sem],
+            device_id=(ctx, exp),
+            device_id_type=pl.DeviceIdType.MESH,
+        )
+
+    def quarter(d):
+        return (e + PLANE_EXP - d) % PLANE_EXP
+
+    def piece(ctx, d, part=None):
+        first = quarter(d) * share
+        if part is None:
+            return normed.at[ctx, pl.ds(pl.multiple_of(first, share), share)]
+        return normed.at[
+            ctx, pl.ds(pl.multiple_of(first + part * (share // 2), share // 2), share // 2)
+        ]
+
+    def head_copy(d):
+        peer = (e + d) % PLANE_EXP
+        src = head_ref.at[pl.ds(pl.multiple_of(peer * share, share), share)]
+        return copy(("head", d), src, zin.at[d], c, peer)
+
+    def z_copy(d):
+        return copy(("z", d), piece(c, 0), piece(c, 0), c, (e + d) % PLANE_EXP)
+
+    def near_copy(pos, d):
+        return copy(("near", pos, d), piece(c, d), piece(c, d), at(pos, k), e)
+
+    def far_copy(pos, d):
+        ref = piece(at(3 - pos, k), d, pos - 1)
+        return copy(("far", pos, d), ref, ref, at(pos, k), e)
+
+    def mate_copy(pos, d):
+        ref = piece(at(pos, k), d)
+        return copy(("mate", pos, d), ref, ref, mate, e)
+
+    def core_copy(pos):
+        return copy(("core", pos), moe.at[at(pos, 1 - k)], core_in.at[pos], mate, e)
+
+    def first_copy(axis, pos):
+        lines = pl.ds((axis - 1) * half, half)
+        slot = (axis - 1) * 2 + (pos == 3)
+        return copy(
+            ("first", axis, pos), moe.at[at(pos, k), lines], first_in.at[slot], at(axis, k), e
+        )
+
+    def second_copy(axis):
+        lines = pl.ds((2 - axis) * half, half)
+        return copy(
+            ("second", axis), moe.at[at(axis, k), lines], second_in.at[2 - axis], at(axis, k), e
+        )
+
+    def out_copy(d):
+        peer = (e + d) % PLANE_EXP
+        return copy(("out", d), stage.at[peer], zout.at[d], c, peer)
+
+    load_gu = pltpu.make_async_copy(gu_hbm, gu, load_sems.at[0])
+    load_down = pltpu.make_async_copy(down_hbm, down, load_sems.at[1])
+    load_gu.start()
+    load_down.start()
+    barrier = pltpu.get_barrier_semaphore()
+    friends = [(mate, e), (at(1, k), e), (at(2, k), e)]
+    friends += [(c, (e + d) % PLANE_EXP) for d in (1, 2, 3)]
+    for friend in friends:
+        pl.semaphore_signal(
+            barrier, inc=1, device_id=friend, device_id_type=pl.DeviceIdType.MESH
+        )
+    pl.semaphore_wait(barrier, len(friends))
+
+    for d in (2, 1, 3):
+        head_copy(d).start()
+    own_lines = pl.ds(pl.multiple_of(e * share, share), share)
+    summed = hidden_ref[...].astype(jnp.float32) + head_ref[own_lines, :].astype(jnp.float32)
+    for d in (1, 3, 2):
+        head_copy(d).wait_recv()
+        summed = summed + zin[d].astype(jnp.float32)
+    residual[...] = summed
+    mean_square = jnp.mean(summed * summed, axis=1, keepdims=True)
+    normed[c, own_lines, :] = (
+        summed * lax.rsqrt(mean_square + 1e-05) * gain_ref[...]
+    ).astype(jnp.bfloat16)
+
+    for d in (2, 1, 3):
+        z_copy(d).start()
+    for d in (0, 1, 3, 2):
+        if d:
+            z_copy(d).wait_recv()
+        near_copy(1, d).start()
+        near_copy(2, d).start()
+        mate_copy(0, d).start()
+    for d in (0, 1, 3, 2):
+        for pos in (1, 2):
+            near_copy(pos, d).wait_recv()
+            far_copy(3 - pos, d).start()
+            mate_copy(pos, d).start()
+    load_gu.wait()
+    load_down.wait()
+
+    def add_core(pos):
+        core_copy(pos).wait_recv()
+        mine = at(pos, k)
+        moe[mine] = (moe[mine].astype(jnp.float32) + core_in[pos].astype(jnp.float32)).astype(
+            jnp.bfloat16
+        )
+
+    def step(pos, carry):
+        for now in range(4):
+
+            @pl.when(pos == now)
+            def _():
+                if now == 2:
+                    for d in range(PLANE_EXP):
+                        far_copy(1, d).wait_recv()
+                        far_copy(2, d).wait_recv()
+                        mate_copy(3, d).start()
+                for d in range(PLANE_EXP):
+                    mate_copy(now, d).wait_recv()
+
+        for core in range(2):
+            block = at(pos, core)
+            rows[pl.ds(core * cap, cap), :] = jnp.dot(
+                pick_ref[block], normed[block], preferred_element_type=jnp.float32
+            ).astype(jnp.bfloat16)
+        across = (((1,), (1,)), ((), ()))
+        gate = lax.dot_general(rows[...], gu[0], across, preferred_element_type=jnp.float32)
+        up = lax.dot_general(rows[...], gu[1], across, preferred_element_type=jnp.float32)
+        activated = ((up + 1.0) * gate * jax.nn.sigmoid(1.702 * gate)).astype(jnp.bfloat16)
+        rows[...] = jnp.dot(activated, down[...], preferred_element_type=jnp.float32).astype(
+            jnp.bfloat16
+        )
+        for core in range(2):
+            block = at(pos, core)
+            moe[block] = jnp.dot(
+                spread_ref[block],
+                rows[pl.ds(core * cap, cap), :],
+                preferred_element_type=jnp.float32,
+            ).astype(jnp.bfloat16)
+        for now in range(4):
+
+            @pl.when(pos == now)
+            def _():
+                core_copy(now).start()
+                if now == 2:
+                    add_core(1)
+                    first_copy(1, 1).start()
+
+        return carry
+
+    lax.fori_loop(0, 4, step, 0)
+    add_core(2)
+    first_copy(2, 2).start()
+    add_core(3)
+    first_copy(1, 3).start()
+    first_copy(2, 3).start()
+    add_core(0)
+
+    for axis in (1, 2):
+        first_copy(axis, 3).wait_recv()
+        lines = pl.ds((axis - 1) * half, half)
+        block = at(3 - axis, k)
+        moe[block, lines, :] = (
+            moe[block, lines, :].astype(jnp.float32)
+            + first_in[(axis - 1) * 2 + 1].astype(jnp.float32)
+        ).astype(jnp.bfloat16)
+        second_copy(3 - axis).start()
+    for axis in (1, 2):
+        first_copy(axis, axis).wait_recv()
+        lines = pl.ds((axis - 1) * half, half)
+        total[lines, :] = moe[c, lines, :].astype(jnp.float32) + first_in[
+            (axis - 1) * 2
+        ].astype(jnp.float32)
+    total[own_lines, :] = total[own_lines, :] + residual[...]
+    for axis in (1, 2):
+        second_copy(3 - axis).wait_recv()
+        lines = pl.ds((axis - 1) * half, half)
+        total[lines, :] = total[lines, :] + second_in[axis - 1].astype(jnp.float32)
+    for f in range(PLANE_EXP):
+        stage[f] = total[:, f * col : (f + 1) * col].astype(jnp.bfloat16)
+    for d in (2, 1, 3):
+        out_copy(d).start()
+    result = stage[e].astype(jnp.float32)
+    for d in (1, 3, 2):
+        out_copy(d).wait_recv()
+        result = result + zout[d].astype(jnp.float32)
+    out_ref[...] = result.astype(jnp.bfloat16)
+
+    for d in (1, 2, 3):
+        head_copy(d).wait_send()
+        z_copy(d).wait_send()
+        out_copy(d).wait_send()
+    for d in range(PLANE_EXP):
+        for pos in range(4):
+            mate_copy(pos, d).wait_send()
+        for pos in (1, 2):
+            near_copy(pos, d).wait_send()
+            far_copy(pos, d).wait_send()
+    for pos in range(4):
+        core_copy(pos).wait_send()
+    for axis in (1, 2):
+        first_copy(axis, axis).wait_send()
+        first_copy(axis, 3).wait_send()
+        second_copy(axis).wait_send()
+
+
+def plane_layer(head_part, hidden_share, gain, pick, spread, gate_up, down_proj):
+    blk, width = head_part.shape
+    blocks, cap = pick.shape[0], pick.shape[1]
+    units = gate_up.shape[-1]
+    share, col = blk // PLANE_EXP, width // PLANE_EXP
+    kind = jnp.bfloat16
+    copies = 64
+    return pl.pallas_call(
+        layer_kernel,
+        out_shape=jax.ShapeDtypeStruct((blk, col), kind),
+        in_specs=[pl.BlockSpec(memory_space=pltpu.VMEM)] * 5
+        + [pl.BlockSpec(memory_space=pl.ANY)] * 2,
+        out_specs=pl.BlockSpec(memory_space=pltpu.VMEM),
+        scratch_shapes=[
+            pltpu.VMEM((2, units, width), kind),
+            pltpu.VMEM((units, width), kind),
+            pltpu.VMEM((PLANE_EXP, share, width), kind),
+            pltpu.VMEM((share, width), jnp.float32),
+            pltpu.VMEM((blocks, blk, width), kind),
+            pltpu.VMEM((2 * cap, width), kind),
+            pltpu.VMEM((blocks, blk, width), kind),
+            pltpu.VMEM((4, blk, width), kind),
+            pltpu.VMEM((4, blk // 2, width), kind),
+            pltpu.VMEM((2, blk // 2, width), kind),
+            pltpu.VMEM((blk, width), jnp.float32),
+            pltpu.VMEM((PLANE_EXP, blk, col), kind),
+            pltpu.VMEM((PLANE_EXP, blk, col), kind),
+            pltpu.SemaphoreType.DMA((copies,)),
+            pltpu.SemaphoreType.DMA((copies,)),
+            pltpu.SemaphoreType.DMA((2,)),
+        ],
+        compiler_params=pltpu.CompilerParams(
+            collective_id=0, has_side_effects=True, vmem_limit_bytes=58 * 1024 * 1024
+        ),
+    )(
+        head_part,
+        hidden_share,
+        gain.reshape(1, width),
+        pick,
+        spread,
+        gate_up[0].transpose(1, 2, 0),
+        down_proj[0],
+    )
 
 
 def per_device(
@@ -139,17 +418,26 @@
     head_part = jnp.dot(attended, out_proj, preferred_element_type=jnp.float32)
     share_rows = tok_rows // exp_count
     my_row = lax.axis_index("exp") * share_rows
-    residual = lax.dynamic_slice_in_dim(hidden_in, my_row, share_rows, 0).astype(
-        jnp.float32
-    ) + lax.psum_scatter(
+    hidden_share = lax.dynamic_slice_in_dim(hidden_in, my_row, share_rows, 0)
+    n_experts = gate_up.shape[0] * ctx_count
+    capacity = max(2, tok_rows * top_count * 5 // (4 * n_experts))
+    pick, weighted = routing_matrices(all_ids, all_gates, ctx_count, tok_rows, capacity)
+    if ctx_count == PLANE_CTX and exp_count == PLANE_EXP:
+        return plane_layer(
+            head_part.astype(jnp.bfloat16),
+            hidden_share,
+            norm_gain,
+            pick,
+            weighted.transpose(0, 2, 1),
+            gate_up,
+            down_proj,
+        )
+    residual = hidden_share.astype(jnp.float32) + lax.psum_scatter(
         head_part.astype(jnp.bfloat16), "exp", scatter_dimension=0, tiled=True
     ).astype(jnp.float32)
     mean_square = jnp.mean(residual * residual, axis=1, keepdims=True)
     normed = (residual * lax.rsqrt(mean_square + 1e-05) * norm_gain[None, :]).astype(jnp.bfloat16)
     all_normed = lax.all_gather(normed, ("ctx", "exp"), axis=0, tiled=True)
-    n_experts = gate_up.shape[0] * ctx_count
-    capacity = max(2, tok_rows * top_count * 5 // (4 * n_experts))
-    pick, weighted = routing_matrices(all_ids, all_gates, ctx_count, tok_rows, capacity)
     expert_rows = jnp.einsum(
         "bst,btd->bsd",
         pick,

time: 261 us -> 147 us (0.56)
  waiting for transfers between devices: 169 us -> 0 us
  Pallas kernels: 0 us -> 113 us
  matrix products: 32.7 us -> 5.1 us
  between operations: 13.4 us -> 0.14 us
  local copies, waits for them, and re-layouts: 22.7 us -> 11.2 us
  other arithmetic: 10.3 us -> 6.2 us
    pallas_call x0 -> x1, Pallas kernels: none -> 113 us  [plane_layer(): pl.pallas_call(layer_kernel, out_shape=jax.ShapeDtypeStruct((blk, col), k...]
    reduce_scatter x2 -> x0, waiting for transfers between devices: 79.1 us -> none  [the longest x1 59.4 us: per_device(): lax.psum_scatter(spread.reshape(ctx_count * tok_rows, D), 'ctx', scatter_...]
    all_gather x1 -> x0, waiting for transfers between devices: 66.3 us -> none  [per_device(): all_normed = lax.all_gather(normed, ('ctx', 'exp'), axis=0, tiled=True)]
    dot_general x4 -> x0, matrix products: 25.6 us -> none  [the longest x1 9.47 us: per_device(): jnp.dot(expert_rows, gate_up.reshape(D, 2 * unit_count), preferred_elemen...]
    unnamed x5 -> x0, waiting for transfers between devices: 23.1 us -> none
    convert_element_type x2 -> x1, local copies, waits for them, and re-layouts: 14.6 us -> 2.26 us  [per_device(): head_part.astype(jnp.bfloat16)]
  transfers between devices with their start and end apart: 4 -> 0, of which waited for: 4 -> 0; matrix products, arithmetic and copies ran while one was open for 2% -> 0% of each run, Pallas kernels for 0% -> 0%
where the time goes in v2:
time: 147 us; the launch traced here: 146 us
  Pallas kernels  113 us (77%)
  local copies, waits for them, and re-layouts  11.2 us (8%)
  blocking collectives  10.9 us (7%)
  other arithmetic  6.2 us (4%)
  matrix products  5.1 us (3%)
    pallas_call x1, Pallas kernels, plane_layer(): pl.pallas_call(layer_kernel, out_shape=jax.ShapeDtypeStruct((blk, col), k...  113 us
    all_gather x1, blocking collectives, per_device(): block_part = lax.all_gather(key_value, 'ctx', axis=0, tiled=True)  10.9 us

profile of v2, /device:TPU:0, one launch (start us, length us, event | category | flops | bytes accessed | tf_op | source)
XLA Modules:
  0.0 146.2 jit_solution(8882938433464316275)
XLA Ops:
  0.0 0.0 copy-start
  0.0 0.0 copy-start.2
  0.0 1.0 constant_dynamic-slice_fusion.1
  1.0 0.1 copy.29
  1.2 0.8 fusion.25
  2.0 0.1 copy.30
  2.1 0.8 subtract_convert_fusion.1
  2.8 0.7 convert_element_type.61
  3.5 0.1 concatenate.12
  3.6 10.9 %all_gather.3 = bf16[1024,140]{0,1:T(8,128)(2,1)S(1)} all-gather(bf16[128,140]{0,1:T(8,128)(2,1)S(1)} %concatenate.12), channel_id=1, replica_groups=mesh['ctx'=8,'exp'=4] {'ctx'}, dimensions={0}, use_global_device_ids=true | all-gather | bytes 322560 | tf_op jit(solution)/shard_map/all_gather | solution.py:388
  14.5 0.8 fusion.31
  15.3 1.0 copy.23
  16.4 0.1 iota_compare_fusion.1
  16.5 0.7 fusion.2
  17.2 0.0 copy-done.2
  17.2 0.1 broadcast_maximum_fusion
  17.3 0.9 fusion
  18.2 0.1 multiply_bitcast_fusion
  18.3 2.4 %fusion.10 = bf16[128,8,64]{0,2,1:T(8,128)(2,1)S(1)} fusion(f32[1024,128,8]{1,0,2:T(8,128)S(1)} %get-tuple-element.18, f32[8,128]{1,0:T(8,128)S(1)} %broadcast_maximum_fusion, pred[128,1024]{0,1:T(8,128)(4,1)S(1)} %iota_compare_fusion.1, bf16[1024,140]{0,1:T(8,128)(2,1)S(1)} %all_gather.3, f32[128,8]{0,1:T(8,128)S(1)} %get-tuple-element.14, ...), kind=kOutput, calls=%fused_computation.13 | convolution fusion | flops 808648704 | bytes 4599808 | tf_op jit(solution)/shard_map/hrk,kd->hrd/dot_general | solution.py:408
  20.7 0.0 copy-done
  20.7 0.0 copy-start.1
  20.7 1.8 %convolution_convert_fusion = bf16[128,2880]{0,1:T(8,128)(2,1)} fusion(bf16[512,2880]{0,1:T(8,128)(2,1)S(1)} %copy-done, bf16[128,512]{0,1:T(8,128)(2,1)S(1)} %bitcast.59), kind=kOutput, calls=%fused_computation.4 | convolution fusion | flops 377856000 | bytes 3817472 | tf_op jit(solution)/shard_map/dot_general | solution.py:418
  22.5 2.3 %copy.26.head_ref = bf16[128,2880]{1,0:T(8,128)(2,1)} copy(bf16[128,2880]{0,1:T(8,128)(2,1)} %convolution_convert_fusion) | data formatting | bytes 1474560 | tf_op jit(solution)/shard_map/convert_element_type | solution.py:427
  24.8 0.1 fusion.19
  24.9 1.2 select_convert_fusion.spread_ref
  26.1 0.7 fusion.13.pick_ref
  26.9 2.3 %constant_dynamic-slice_fusion = bf16[32,2880]{0,1:T(8,128)(2,1)} fusion(bf16[128,2880]{0,1:T(8,128)(2,1)} %param.13, s32[]{:T(128)S(6)} %select_n.32), kind=kLoop, calls=%fused_computation.66 | loop fusion | bytes 368644 | tf_op jit(solution)/shard_map/dynamic_slice | solution.py:421
  29.1 2.0 %copy.31.hidden_ref = bf16[32,2880]{1,0:T(8,128)(2,1)} copy(bf16[32,2880]{0,1:T(8,128)(2,1)} %constant_dynamic-slice_fusion) | data formatting | bytes 368640
  31.1 0.0 copy-done.1
  31.2 0.6 reshape.273.gain_ref
  31.8 112.7 %shard_map.127 = bf16[128,720]{1,0:T(8,128)(2,1)} custom-call(bf16[128,2880]{1,0:T(8,128)(2,1)} %copy.26.head_ref, bf16[32,2880]{1,0:T(8,128)(2,1)} %copy.31.hidden_ref, f32[1,2880]{1,0:T(1,128)} %reshape.273.gain_ref, bf16[8,80,128]{2,1,0:T(8,128)(2,1)} %fusion.13.pick_ref, bf16[8,128,80]{2,1,0:T(8,128)(2,1)} %select_convert_fusion.spread_ref, ...), custom_call_target="tpu_custom_call" | custom-call | tf_op jit(solution)/shard_map/pallas_call | solution.py:311
  144.5 1.7 %copy.27 = bf16[128,720]{0,1:T(8,128)(2,1)} copy(bf16[128,720]{1,0:T(8,128)(2,1)} %shard_map.127) | data formatting | bytes 368640 | tf_op jit(solution)/shard_map/pallas_call | solution.py:311
  (8 shorter events, 0.1 us)
Async XLA Ops:
  0.0 20.7 %copy-start = (bf16[512,2880]{0,1:T(8,128)(2,1)S(1)}, bf16[512,2880]{0,1:T(8,128)(2,1)}, u32[]{:S(2)}) copy-start(bf16[512,2880]{0,1:T(8,128)(2,1)} %param.18) | copy-start | bytes 8847364
  0.0 17.2 %copy-start.2 = (f32[8]{0:T(128)S(1)}, f32[8]{0:T(128)}, u32[]{:S(2)}) copy-start(f32[8]{0:T(128)} %param.17) | copy-start | bytes 100
  20.7 10.5 %copy-start.1 = (f32[2880]{0:T(1024)S(1)}, f32[2880]{0:T(1024)}, u32[]{:S(2)}) copy-start(f32[2880]{0:T(1024)} %param.19) | copy-start | bytes 34564

commit v3 on v2

--- a/solution.py
+++ b/solution.py
@@ -74,15 +74,16 @@
 
 
 def layer_kernel(
-    head_ref, hidden_ref, gain_ref, pick_ref, spread_ref, gu_hbm, down_hbm, out_ref,
-    gu, down, zin, residual, normed, rows, moe, core_in, first_in, second_in, total, stage, zout,
+    attended_ref, hidden_ref, gain_ref, pick_ref, spread_ref, proj_hbm, gu_hbm, down_hbm, out_ref,
+    proj, gu, down, head, hidden, zin, residual, normed, rows, moe, core_in, first_in, corner_in, second_in, total, stage, zout,
     send_sems, recv_sems, load_sems,
 ):
     c, e = lax.axis_index("ctx"), lax.axis_index("exp")
     y, x, k = c // 4, c // 2 % 2, c % 2
-    blk = head_ref.shape[0]
+    blk = attended_ref.shape[0]
     share = blk // PLANE_EXP
     half = blk // 2
+    sub = half // 2
     cap = pick_ref.shape[1]
     col = out_ref.shape[1]
 
@@ -116,7 +117,7 @@
 
     def head_copy(d):
         peer = (e + d) % PLANE_EXP
-        src = head_ref.at[pl.ds(pl.multiple_of(peer * share, share), share)]
+        src = head.at[pl.ds(pl.multiple_of(peer * share, share), share)]
         return copy(("head", d), src, zin.at[d], c, peer)
 
     def z_copy(d):
@@ -136,27 +137,30 @@
     def core_copy(pos):
         return copy(("core", pos), moe.at[at(pos, 1 - k)], core_in.at[pos], mate, e)
 
-    def first_copy(axis, pos):
+    def lines_of(axis, part):
+        return pl.ds((axis - 1) * half + part * sub, sub)
+
+    def first_copy(axis):
         lines = pl.ds((axis - 1) * half, half)
-        slot = (axis - 1) * 2 + (pos == 3)
-        return copy(
-            ("first", axis, pos), moe.at[at(pos, k), lines], first_in.at[slot], at(axis, k), e
-        )
-
-    def second_copy(axis):
-        lines = pl.ds((2 - axis) * half, half)
-        return copy(
-            ("second", axis), moe.at[at(axis, k), lines], second_in.at[2 - axis], at(axis, k), e
-        )
-
-    def out_copy(d):
+        src = moe.at[at(axis, k), lines]
+        return copy(("first", axis), src, first_in.at[axis - 1], at(axis, k), e)
+
+    def corner_copy(axis, part):
+        src = moe.at[at(3, k), lines_of(axis, part)]
+        return copy(("corner", axis, part), src, corner_in.at[axis - 1, part], at(axis, k), e)
+
+    def second_copy(axis, part):
+        src = moe.at[at(axis, k), lines_of(3 - axis, part)]
+        return copy(("second", axis, part), src, second_in.at[axis - 1, part], at(axis, k), e)
+
+    def out_copy(d, part):
         peer = (e + d) % PLANE_EXP
-        return copy(("out", d), stage.at[peer], zout.at[d], c, peer)
-
+        return copy(("out", d, part), stage.at[peer, part], zout.at[d, part], c, peer)
+
+    load_proj = pltpu.make_async_copy(proj_hbm, proj, load_sems.at[2])
+    load_proj.start()
     load_gu = pltpu.make_async_copy(gu_hbm, gu, load_sems.at[0])
     load_down = pltpu.make_async_copy(down_hbm, down, load_sems.at[1])
-    load_gu.start()
-    load_down.start()
     barrier = pltpu.get_barrier_semaphore()
     friends = [(mate, e), (at(1, k), e), (at(2, k), e)]
     friends += [(c, (e + d) % PLANE_EXP) for d in (1, 2, 3)]
@@ -166,10 +170,19 @@
         )
     pl.semaphore_wait(barrier, len(friends))
 
+    load_proj.wait()
+    load_gu.start()
+    load_down.start()
+    across = (((1,), (1,)), ((), ()))
+    head[...] = (
+        lax.dot_general(proj[...], attended_ref[...], across, preferred_element_type=jnp.float32)
+        .T.astype(jnp.bfloat16)
+    )
     for d in (2, 1, 3):
         head_copy(d).start()
+    hidden[...] = hidden_ref[...].astype(jnp.float32).T
     own_lines = pl.ds(pl.multiple_of(e * share, share), share)
-    summed = hidden_ref[...].astype(jnp.float32) + head_ref[own_lines, :].astype(jnp.float32)
+    summed = hidden[own_lines, :] + head[own_lines, :].astype(jnp.float32)
     for d in (1, 3, 2):
         head_copy(d).wait_recv()
         summed = summed + zin[d].astype(jnp.float32)
@@ -215,78 +228,89 @@
                 for d in range(PLANE_EXP):
                     mate_copy(now, d).wait_recv()
 
-        for core in range(2):
+        for slot, core in enumerate((1 - k, k)):
             block = at(pos, core)
-            rows[pl.ds(core * cap, cap), :] = jnp.dot(
+            rows[slot * cap : (slot + 1) * cap, :] = jnp.dot(
                 pick_ref[block], normed[block], preferred_element_type=jnp.float32
             ).astype(jnp.bfloat16)
-        across = (((1,), (1,)), ((), ()))
-        gate = lax.dot_general(rows[...], gu[0], across, preferred_element_type=jnp.float32)
-        up = lax.dot_general(rows[...], gu[1], across, preferred_element_type=jnp.float32)
-        activated = ((up + 1.0) * gate * jax.nn.sigmoid(1.702 * gate)).astype(jnp.bfloat16)
+        gate = lax.dot_general(gu[0], rows[...], across, preferred_element_type=jnp.float32)
+        up = lax.dot_general(gu[1], rows[...], across, preferred_element_type=jnp.float32)
+        activated = ((up + 1.0) * gate * jax.nn.sigmoid(1.702 * gate)).T.astype(jnp.bfloat16)
         rows[...] = jnp.dot(activated, down[...], preferred_element_type=jnp.float32).astype(
             jnp.bfloat16
         )
-        for core in range(2):
+        for slot, core in enumerate((1 - k, k)):
             block = at(pos, core)
             moe[block] = jnp.dot(
                 spread_ref[block],
-                rows[pl.ds(core * cap, cap), :],
+                rows[slot * cap : (slot + 1) * cap, :],
                 preferred_element_type=jnp.float32,
             ).astype(jnp.bfloat16)
-        for now in range(4):
-
-            @pl.when(pos == now)
-            def _():
-                core_copy(now).start()
-                if now == 2:
-                    add_core(1)
-                    first_copy(1, 1).start()
+            if slot == 0:
+                for now in range(4):
+
+                    @pl.when(pos == now)
+                    def _():
+                        core_copy(now).start()
+
+        @pl.when(pos == 2)
+        def _():
+            add_core(1)
+            first_copy(1).start()
 
         return carry
 
     lax.fori_loop(0, 4, step, 0)
     add_core(2)
-    first_copy(2, 2).start()
+    first_copy(2).start()
+    add_core(0)
+    total[...] = moe[c].astype(jnp.float32)
+    total[own_lines, :] = total[own_lines, :] + residual[...]
     add_core(3)
-    first_copy(1, 3).start()
-    first_copy(2, 3).start()
-    add_core(0)
-
+    for part in range(2):
+        for axis in (1, 2):
+            corner_copy(axis, part).start()
+
+    for part in range(2):
+        for axis in (1, 2):
+            corner_copy(axis, part).wait_recv()
+            lines = lines_of(axis, part)
+            block = at(3 - axis, k)
+            moe[block, lines, :] = (
+                moe[block, lines, :].astype(jnp.float32)
+                + corner_in[axis - 1, part].astype(jnp.float32)
+            ).astype(jnp.bfloat16)
+            second_copy(3 - axis, part).start()
     for axis in (1, 2):
-        first_copy(axis, 3).wait_recv()
+        first_copy(axis).wait_recv()
         lines = pl.ds((axis - 1) * half, half)
-        block = at(3 - axis, k)
-        moe[block, lines, :] = (
-            moe[block, lines, :].astype(jnp.float32)
-            + first_in[(axis - 1) * 2 + 1].astype(jnp.float32)
-        ).astype(jnp.bfloat16)
-        second_copy(3 - axis).start()
-    for axis in (1, 2):
-        first_copy(axis, axis).wait_recv()
-        lines = pl.ds((axis - 1) * half, half)
-        total[lines, :] = moe[c, lines, :].astype(jnp.float32) + first_in[
-            (axis - 1) * 2
-        ].astype(jnp.float32)
-    total[own_lines, :] = total[own_lines, :] + residual[...]
-    for axis in (1, 2):
-        second_copy(3 - axis).wait_recv()
-        lines = pl.ds((axis - 1) * half, half)
-        total[lines, :] = total[lines, :] + second_in[axis - 1].astype(jnp.float32)
-    for f in range(PLANE_EXP):
-        stage[f] = total[:, f * col : (f + 1) * col].astype(jnp.bfloat16)
-    for d in (2, 1, 3):
-        out_copy(d).start()
-    result = stage[e].astype(jnp.float32)
-    for d in (1, 3, 2):
-        out_copy(d).wait_recv()
-        result = result + zout[d].astype(jnp.float32)
-    out_ref[...] = result.astype(jnp.bfloat16)
+        total[lines, :] = total[lines, :] + first_in[axis - 1].astype(jnp.float32)
+    for part in range(2):
+        for axis in (1, 2):
+            second_copy(3 - axis, part).wait_recv()
+            lines = lines_of(axis, part)
+            full = (total[lines, :] + second_in[2 - axis, part].astype(jnp.float32)).astype(
+                jnp.bfloat16
+            )
+            for f in range(PLANE_EXP):
+                stage[f, part, (axis - 1) * sub : axis * sub, :] = full[:, f * col : (f + 1) * col]
+        for d in (2, 1, 3):
+            out_copy(d, part).start()
+    for part in range(2):
+        result = stage[e, part].astype(jnp.float32)
+        for d in (1, 3, 2):
+            out_copy(d, part).wait_recv()
+            result = result + zout[d, part].astype(jnp.float32)
+        for axis in (1, 2):
+            out_ref[lines_of(axis, part), :] = result[(axis - 1) * sub : axis * sub].astype(
+                jnp.bfloat16
+            )
 
     for d in (1, 2, 3):
         head_copy(d).wait_send()
         z_copy(d).wait_send()
-        out_copy(d).wait_send()
+        for part in range(2):
+            out_copy(d, part).wait_send()
     for d in range(PLANE_EXP):
         for pos in range(4):
             mate_copy(pos, d).wait_send()
@@ -296,13 +320,63 @@
     for pos in range(4):
         core_copy(pos).wait_send()
     for axis in (1, 2):
-        first_copy(axis, axis).wait_send()
-        first_copy(axis, 3).wait_send()
-        second_copy(axis).wait_send()
-
-
-def plane_layer(head_part, hidden_share, gain, pick, spread, gate_up, down_proj):
-    blk, width = head_part.shape
+        first_copy(axis).wait_send()
+        for part in range(2):
+            corner_copy(axis, part).wait_send()
+            second_copy(axis, part).wait_send()
+
+
+def gather_kernel(mine_ref, all_ref, send_sems, recv_sems, own_sem):
+    c, e = lax.axis_index("ctx"), lax.axis_index("exp")
+    count = all_ref.shape[0]
+    own = pltpu.make_async_copy(mine_ref, all_ref.at[c], own_sem)
+    own.start()
+    barrier = pltpu.get_barrier_semaphore()
+    for d in range(1, count):
+        pl.semaphore_signal(
+            barrier,
+            inc=1,
+            device_id=((c + d) % count, e),
+            device_id_type=pl.DeviceIdType.MESH,
+        )
+    pl.semaphore_wait(barrier, count - 1)
+    copies = [
+        pltpu.make_async_remote_copy(
+            src_ref=mine_ref,
+            dst_ref=all_ref.at[c],
+            send_sem=send_sems.at[d],
+            recv_sem=recv_sems.at[d],
+            device_id=((c + d) % count, e),
+            device_id_type=pl.DeviceIdType.MESH,
+        )
+        for d in range(1, count)
+    ]
+    for item in copies:
+        item.start()
+    own.wait()
+    for item in copies:
+        item.wait()
+
+
+def plane_gather(mine):
+    return pl.pallas_call(
+        gather_kernel,
+        out_shape=jax.ShapeDtypeStruct((PLANE_CTX, *mine.shape), mine.dtype),
+        in_specs=[pl.BlockSpec(memory_space=pltpu.VMEM)],
+        out_specs=pl.BlockSpec(memory_space=pltpu.VMEM),
+        scratch_shapes=[
+            pltpu.SemaphoreType.DMA((PLANE_CTX,)),
+            pltpu.SemaphoreType.DMA((PLANE_CTX,)),
+            pltpu.SemaphoreType.DMA,
+        ],
+        compiler_params=pltpu.CompilerParams(
+            collective_id=1, has_side_effects=True, vmem_limit_bytes=8 * 1024 * 1024
+        ),
+    )(mine)
+
+
+def plane_layer(attended, hidden_in, gain, pick, spread, out_proj, gate_up, down_proj):
+    blk, width = hidden_in.shape
     blocks, cap = pick.shape[0], pick.shape[1]
     units = gate_up.shape[-1]
     share, col = blk // PLANE_EXP, width // PLANE_EXP
@@ -312,35 +386,40 @@
         layer_kernel,
         out_shape=jax.ShapeDtypeStruct((blk, col), kind),
         in_specs=[pl.BlockSpec(memory_space=pltpu.VMEM)] * 5
-        + [pl.BlockSpec(memory_space=pl.ANY)] * 2,
+        + [pl.BlockSpec(memory_space=pl.ANY)] * 3,
         out_specs=pl.BlockSpec(memory_space=pltpu.VMEM),
         scratch_shapes=[
+            pltpu.VMEM((width, out_proj.shape[0]), kind),
             pltpu.VMEM((2, units, width), kind),
             pltpu.VMEM((units, width), kind),
+            pltpu.VMEM((blk, width), kind),
+            pltpu.VMEM((blk, width), jnp.float32),
             pltpu.VMEM((PLANE_EXP, share, width), kind),
             pltpu.VMEM((share, width), jnp.float32),
             pltpu.VMEM((blocks, blk, width), kind),
             pltpu.VMEM((2 * cap, width), kind),
             pltpu.VMEM((blocks, blk, width), kind),
             pltpu.VMEM((4, blk, width), kind),
-            pltpu.VMEM((4, blk // 2, width), kind),
             pltpu.VMEM((2, blk // 2, width), kind),
+            pltpu.VMEM((2, 2, blk // 4, width), kind),
+            pltpu.VMEM((2, 2, blk // 4, width), kind),
             pltpu.VMEM((blk, width), jnp.float32),
-            pltpu.VMEM((PLANE_EXP, blk, col), kind),
-            pltpu.VMEM((PLANE_EXP, blk, col), kind),
+            pltpu.VMEM((PLANE_EXP, 2, blk // 2, col), kind),
+            pltpu.VMEM((PLANE_EXP, 2, blk // 2, col), kind),
             pltpu.SemaphoreType.DMA((copies,)),
             pltpu.SemaphoreType.DMA((copies,)),
-            pltpu.SemaphoreType.DMA((2,)),
+            pltpu.SemaphoreType.DMA((3,)),
         ],
         compiler_params=pltpu.CompilerParams(
             collective_id=0, has_side_effects=True, vmem_limit_bytes=58 * 1024 * 1024
         ),
     )(
-        head_part,
-        hidden_share,
+        attended,
+        hidden_in.T,
         gain.reshape(1, width),
         pick,
         spread,
+        out_proj.T,
         gate_up[0].transpose(1, 2, 0),
         down_proj[0],
     )
@@ -385,7 +464,13 @@
     top_count = expert_ids.shape[1]
     key_value = jnp.concatenate([key_rot, value_block, ids_part, gate_high, gate_low], axis=1)
     score_scale = 1.0 / math.sqrt(HEAD_SIZE)
-    block_part = lax.all_gather(key_value, "ctx", axis=0, tiled=True)
+    in_plane = ctx_count == PLANE_CTX and exp_count == PLANE_EXP
+    if in_plane:
+        width = key_value.shape[1]
+        padded = jnp.pad(key_value, ((0, 0), (0, -width % 128)))
+        block_part = plane_gather(padded).reshape(ctx_count * tok_rows, -1)[:, :width]
+    else:
+        block_part = lax.all_gather(key_value, "ctx", axis=0, tiled=True)
     routing = block_part[:, 2 * HEAD_SIZE :].astype(jnp.float32)
     all_ids = routing[:, :top_count]
     all_gates = routing[:, top_count : 2 * top_count] + routing[:, 2 * top_count :]
@@ -415,23 +500,24 @@
         .reshape(tok_rows, local_heads * HEAD_SIZE)
         .astype(jnp.bfloat16)
     )
-    head_part = jnp.dot(attended, out_proj, preferred_element_type=jnp.float32)
     share_rows = tok_rows // exp_count
     my_row = lax.axis_index("exp") * share_rows
-    hidden_share = lax.dynamic_slice_in_dim(hidden_in, my_row, share_rows, 0)
     n_experts = gate_up.shape[0] * ctx_count
     capacity = max(2, tok_rows * top_count * 5 // (4 * n_experts))
     pick, weighted = routing_matrices(all_ids, all_gates, ctx_count, tok_rows, capacity)
-    if ctx_count == PLANE_CTX and exp_count == PLANE_EXP:
+    if in_plane:
         return plane_layer(
-            head_part.astype(jnp.bfloat16),
-            hidden_share,
+            attended,
+            hidden_in,
             norm_gain,
             pick,
             weighted.transpose(0, 2, 1),
+            out_proj,
             gate_up,
             down_proj,
         )
+    head_part = jnp.dot(attended, out_proj, preferred_element_type=jnp.float32)
+    hidden_share = lax.dynamic_slice_in_dim(hidden_in, my_row, share_rows, 0)
     residual = hidden_share.astype(jnp.float32) + lax.psum_scatter(
         head_part.astype(jnp.bfloat16), "exp", scatter_dimension=0, tiled=True
     ).astype(jnp.float32)

time: 147 us -> 141 us (0.959)
  Pallas kernels: 113 us -> 125 us
  blocking collectives: 10.9 us -> 0 us
  local copies, waits for them, and re-layouts: 11.2 us -> 4.75 us
  matrix products: 5.1 us -> 3.32 us
  other arithmetic: 6.2 us -> 7.84 us
    all_gather x1 -> x0, blocking collectives: 10.9 us -> none  [per_device(): block_part = lax.all_gather(key_value, 'ctx', axis=0, tiled=True)]
    pallas_call x0 -> x1, Pallas kernels: none -> 10.5 us  [plane_gather(): pl.pallas_call(gather_kernel, out_shape=jax.ShapeDtypeStruct((PLANE_CTX,...]
    dynamic_slice x1 -> x0, local copies, waits for them, and re-layouts: 2.26 us -> none  [per_device(): hidden_share = lax.dynamic_slice_in_dim(hidden_in, my_row, share_rows, 0)]
    unnamed x9 -> x6, local copies, waits for them, and re-layouts: 2.21 us -> 0.01 us
    dot_general x1 -> x0, matrix products: 1.82 us -> none  [per_device(): head_part = jnp.dot(attended, out_proj, preferred_element_type=jnp.float32)]
where the time goes in v3:
time: 141 us
  Pallas kernels  125 us (89%)
  other arithmetic  7.84 us (6%)
  local copies, waits for them, and re-layouts  4.75 us (3%)
  matrix products  3.32 us (2%)
    pallas_call x1, Pallas kernels, plane_layer(): pl.pallas_call(layer_kernel, out_shape=jax.ShapeDtypeStruct((blk, col), k...  114 us
    pallas_call x1, Pallas kernels, plane_gather(): pl.pallas_call(gather_kernel, out_shape=jax.ShapeDtypeStruct((PLANE_CTX,...  10.5 us

profile of v3, /device:TPU:0, one launch (start us, length us, event | category | flops | bytes accessed | tf_op | source)
XLA Modules:
  0.0 140.7 jit_solution(7615957135012514057)
XLA Ops:
  0.0 0.0 copy-start
  0.0 0.0 copy-start.2
  0.0 0.1 iota_compare_fusion.1
  0.1 1.0 copy.37
  1.1 0.8 fusion.33
  2.0 0.8 bitcast_convert_fusion
  2.8 1.0 fusion.24
  3.8 0.1 maximum_bitcast_fusion
  3.9 0.0 copy-done
  3.9 0.1 constant_dynamic-slice_fusion
  4.0 0.7 convert_element_type.59
  4.7 0.1 copy.33
  4.8 0.8 subtract_convert_fusion.1
  5.6 0.1 copy.34
  5.7 0.1 copy.35
  5.9 0.1 concatenate.12
  6.0 10.5 %shard_map.127 = bf16[8,128,256]{2,1,0:T(8,128)(2,1)S(1)} custom-call(bf16[128,256]{1,0:T(8,128)(2,1)S(1)} %pad.4.mine_ref), custom_call_target="tpu_custom_call" | custom-call | tf_op jit(solution)/shard_map/pallas_call | solution.py:362
  16.5 0.7 fusion.2
  17.2 0.0 copy-done.2
  17.2 0.1 broadcast_maximum_fusion
  17.3 0.9 fusion
  18.2 0.0 copy-start.1
  18.2 0.1 multiply_bitcast_fusion
  18.3 2.5 %fusion.10 = bf16[128,8,64]{0,2,1:T(8,128)(2,1)S(1)} fusion(f32[1024,128,8]{1,0,2:T(8,128)S(1)} %get-tuple-element.18, f32[8,128]{1,0:T(8,128)S(1)} %broadcast_maximum_fusion, pred[128,1024]{0,1:T(8,128)(4,1)S(1)} %iota_compare_fusion.1, bf16[1024,256]{1,0:T(8,128)(2,1)S(1)} %bitcast.60, f32[128,8]{0,1:T(8,128)S(1)} %get-tuple-element.14, ...), kind=kOutput, calls=%fused_computation.12 | convolution fusion | flops 808648704 | bytes 4730880 | tf_op jit(solution)/shard_map/hrk,kd->hrd/dot_general | solution.py:493
  20.8 0.8 copy.40.attended_ref
  21.5 0.0 copy-done.1
  21.5 0.6 reshape.277.gain_ref
  22.2 0.6 fusion.12
  22.8 0.1 fusion.31
  22.9 0.7 fusion.15.pick_ref
  23.6 1.2 select_convert_fusion.spread_ref
  24.8 114.2 %shard_map.128 = bf16[128,720]{1,0:T(8,128)(2,1)} custom-call(bf16[128,512]{1,0:T(8,128)(2,1)} %copy.40.attended_ref, bf16[2880,128]{1,0:T(8,128)(2,1)} %bitcast.66, f32[1,2880]{1,0:T(1,128)} %reshape.277.gain_ref, bf16[8,80,128]{2,1,0:T(8,128)(2,1)} %fusion.15.pick_ref, bf16[8,128,80]{2,1,0:T(8,128)(2,1)} %select_convert_fusion.spread_ref, ...), custom_call_target="tpu_custom_call" | custom-call | tf_op jit(solution)/shard_map/pallas_call | solution.py:385
  139.0 1.7 %copy.41 = bf16[128,720]{0,1:T(8,128)(2,1)} copy(bf16[128,720]{1,0:T(8,128)(2,1)} %shard_map.128) | data formatting | bytes 368640 | tf_op jit(solution)/shard_map/pallas_call | solution.py:385
  (5 shorter events, 0.1 us)
Async XLA Ops:
  0.0 3.9 %copy-start = (bf16[128,256]{1,0:T(8,128)(2,1)S(1)}, bf16[128,256]{1,0:T(8,128)(2,1)}, u32[]{:S(2)}) copy-start(bf16[128,256]{1,0:T(8,128)(2,1)} %param.16) | copy-start | bytes 196612
  0.0 17.2 %copy-start.2 = (f32[8]{0:T(128)S(1)}, f32[8]{0:T(128)}, u32[]{:S(2)}) copy-start(f32[8]{0:T(128)} %param.17) | copy-start | bytes 100
  18.2 3.4 %copy-start.1 = (f32[2880]{0:T(1024)S(1)}, f32[2880]{0:T(1024)}, u32[]{:S(2)}) copy-start(f32[2880]{0:T(1024)} %param.19) | copy-start | bytes 34564

commit v4 on v1

--- a/solution.py
+++ b/solution.py
@@ -1,9 +1,12 @@
+import functools
 import math
 
 import jax
 import jax.numpy as jnp
 import numpy as np
 from jax import lax
+from jax.experimental import pallas as pl
+from jax.experimental.pallas import tpu as pltpu
 from jax.sharding import PartitionSpec as P
 
 D = 2880
@@ -65,6 +68,348 @@
     pick = hit.astype(jnp.bfloat16)
     weighted = jnp.where(hit, gate[:, None, :], 0.0).astype(jnp.bfloat16)
     return pick, weighted
+
+
+PLANE_CTX = 8
+PLANE_EXP = 4
+
+
+def layer_kernel(
+    attended_ref, hidden_ref, gain_ref, gate_ref, proj_hbm, gu_hbm, down_hbm, out_ref,
+    proj, gu, down, head, hidden, zin, residual, normed, moe, core_in, first_in, corner_in,
+    second_in, total, stage, zout, send_sems, recv_sems, load_sems,
+):
+    c, e = lax.axis_index("ctx"), lax.axis_index("exp")
+    y, x, k = c // 4, c // 2 % 2, c % 2
+    blk, width = head.shape
+    share = blk // PLANE_EXP
+    half = share // 2
+    col = out_ref.shape[1]
+
+    def at(pos, core):
+        return (y + pos // 2) % 2 * 4 + (x + pos % 2) % 2 * 2 + core
+
+    mate = at(0, 1 - k)
+    ids = {}
+
+    def copy(name, src, dst, ctx, exp):
+        sem = ids.setdefault(name, len(ids))
+        return pltpu.make_async_remote_copy(
+            src_ref=src,
+            dst_ref=dst,
+            send_sem=send_sems.at[sem],
+            recv_sem=recv_sems.at[sem],
+            device_id=(ctx, exp),
+            device_id_type=pl.DeviceIdType.MESH,
+        )
+
+    def quarter(d):
+        return (e + PLANE_EXP - d) % PLANE_EXP
+
+    def lines(axis):
+        return pl.ds((axis - 1) * half, half)
+
+    def head_copy(d):
+        peer = (e + d) % PLANE_EXP
+        src = head.at[pl.ds(pl.multiple_of(peer * share, share), share)]
+        return copy(("head", d), src, zin.at[d], c, peer)
+
+    def z_copy(d):
+        ref = normed.at[e, c]
+        return copy(("z", d), ref, ref, c, (e + d) % PLANE_EXP)
+
+    def near_copy(pos, d):
+        ref = normed.at[quarter(d), c]
+        return copy(("near", pos, d), ref, ref, at(pos, k), e)
+
+    def far_copy(pos, d):
+        ref = normed.at[quarter(d), at(3 - pos, k), lines(pos)]
+        return copy(("far", pos, d), ref, ref, at(pos, k), e)
+
+    def mate_copy(pos, d):
+        ref = normed.at[quarter(d), at(pos, k)]
+        return copy(("mate", pos, d), ref, ref, mate, e)
+
+    def core_copy(pos, d):
+        src = moe.at[quarter(d), at(pos, 1 - k)]
+        return copy(("core", pos, d), src, core_in.at[d, pos], mate, e)
+
+    def first_copy(axis, d):
+        src = moe.at[quarter(d), at(axis, k), lines(axis)]
+        return copy(("first", axis, d), src, first_in.at[d, axis - 1], at(axis, k), e)
+
+    def corner_copy(axis, d):
+        src = moe.at[quarter(d), at(3, k), lines(axis)]
+        return copy(("corner", axis, d), src, corner_in.at[d, axis - 1], at(axis, k), e)
+
+    def second_copy(axis, d):
+        src = moe.at[quarter(d), at(axis, k), lines(3 - axis)]
+        return copy(("second", axis, d), src, second_in.at[d, axis - 1], at(axis, k), e)
+
+    def out_copy(d, j):
+        peer = (e + j) % PLANE_EXP
+        return copy(("out", d, j), stage.at[d, peer], zout.at[j, quarter(d)], c, peer)
+
+    load_proj = pltpu.make_async_copy(proj_hbm, proj, load_sems.at[2])
+    load_proj.start()
+    load_gu = pltpu.make_async_copy(gu_hbm, gu, load_sems.at[0])
+    load_down = pltpu.make_async_copy(down_hbm, down, load_sems.at[1])
+    barrier = pltpu.get_barrier_semaphore()
+    friends = [(mate, e), (at(1, k), e), (at(2, k), e)]
+    friends += [(c, (e + d) % PLANE_EXP) for d in (1, 2, 3)]
+    for friend in friends:
+        pl.semaphore_signal(
+            barrier, inc=1, device_id=friend, device_id_type=pl.DeviceIdType.MESH
+        )
+    pl.semaphore_wait(barrier, len(friends))
+
+    load_proj.wait()
+    load_gu.start()
+    load_down.start()
+    across = (((1,), (1,)), ((), ()))
+    head[...] = (
+        lax.dot_general(proj[...], attended_ref[...], across, preferred_element_type=jnp.float32)
+        .T.astype(jnp.bfloat16)
+    )
+    for d in (2, 1, 3):
+        head_copy(d).start()
+    hidden[...] = hidden_ref[...].astype(jnp.float32).T
+    own_lines = pl.ds(pl.multiple_of(e * share, share), share)
+    summed = hidden[own_lines, :] + head[own_lines, :].astype(jnp.float32)
+    for d in (1, 3, 2):
+        head_copy(d).wait_recv()
+        summed = summed + zin[d].astype(jnp.float32)
+    residual[...] = summed
+    mean_square = jnp.mean(summed * summed, axis=1, keepdims=True)
+    normed[e, c] = (summed * lax.rsqrt(mean_square + 1e-05) * gain_ref[...]).astype(jnp.bfloat16)
+
+    def spread_near(d):
+        near_copy(1, d).start()
+        near_copy(2, d).start()
+        mate_copy(0, d).start()
+
+    def spread_far(d):
+        for pos in (1, 2):
+            near_copy(pos, d).wait_recv()
+            far_copy(3 - pos, d).start()
+            mate_copy(pos, d).start()
+
+    def finish_spread(d):
+        far_copy(1, d).wait_recv()
+        far_copy(2, d).wait_recv()
+        mate_copy(3, d).start()
+        for pos in range(4):
+            mate_copy(pos, d).wait_recv()
+
+    def plus(target, added):
+        target[...] = (target[...].astype(jnp.float32) + added[...].astype(jnp.float32)).astype(
+            jnp.bfloat16
+        )
+
+    def sum_cores(d):
+        for pos in (3, 1, 2, 0):
+            core_copy(pos, d).wait_recv()
+            plus(moe.at[quarter(d), at(pos, k)], core_in.at[d, pos])
+            if pos == 3:
+                corner_copy(1, d).start()
+                corner_copy(2, d).start()
+            elif pos:
+                first_copy(pos, d).start()
+
+    def sum_corners(d):
+        for axis in (1, 2):
+            corner_copy(axis, d).wait_recv()
+            plus(
+                moe.at[quarter(d), at(3 - axis, k), lines(axis)],
+                corner_in.at[d, axis - 1],
+            )
+            second_copy(3 - axis, d).start()
+
+    def finish_sum(d):
+        for axis in (1, 2):
+            first_copy(axis, d).wait_recv()
+            second_copy(3 - axis, d).wait_recv()
+            total[lines(axis), :] = (
+                moe[quarter(d), c, lines(axis), :].astype(jnp.float32)
+                + first_in[d, axis - 1].astype(jnp.float32)
+                + second_in[d, 2 - axis].astype(jnp.float32)
+            )
+        full = total[...] + residual[...] if d == 0 else total[...]
+        for f in range(PLANE_EXP):
+            stage[d, f] = full[:, f * col : (f + 1) * col].astype(jnp.bfloat16)
+        for j in (2, 1, 3):
+            out_copy(d, j).start()
+
+    for d in (2, 1, 3):
+        z_copy(d).start()
+    spread_near(0)
+
+    def before(d):
+        spread_far(d)
+        if d + 1 < PLANE_EXP:
+            z_copy(d + 1).wait_recv()
+            spread_near(d + 1)
+        finish_spread(d)
+        if d == 0:
+            load_gu.wait()
+            load_down.wait()
+        if d >= 1:
+            sum_cores(d - 1)
+        if d >= 2:
+            finish_sum(d - 2)
+
+    def after(d):
+        for pos in (3, 1, 2, 0):
+            core_copy(pos, d).start()
+        if d >= 1:
+            sum_corners(d - 1)
+
+    def step(d, carry):
+        for now in range(PLANE_EXP):
+            pl.when(d == now)(functools.partial(before, now))
+        part = quarter(d)
+        tokens = normed[part].reshape(-1, width)
+        gate = lax.dot_general(gu[0], tokens, across, preferred_element_type=jnp.float32)
+        up = lax.dot_general(gu[1], tokens, across, preferred_element_type=jnp.float32)
+        activated = (up + 1.0) * gate * jax.nn.sigmoid(1.702 * gate) * gate_ref[part]
+        moe[part] = (
+            jnp.dot(
+                activated.T.astype(jnp.bfloat16), down[...], preferred_element_type=jnp.float32
+            )
+            .astype(jnp.bfloat16)
+            .reshape(-1, share, width)
+        )
+        for now in range(PLANE_EXP):
+            pl.when(d == now)(functools.partial(after, now))
+        return carry
+
+    lax.fori_loop(0, PLANE_EXP, step, 0)
+    last = PLANE_EXP - 1
+    sum_cores(last)
+    finish_sum(last - 1)
+    sum_corners(last)
+    finish_sum(last)
+    for d in range(PLANE_EXP):
+        zout[0, quarter(d)] = stage[d, e]
+        for j in (1, 2, 3):
+            out_copy(d, j).wait_recv()
+    for q in range(PLANE_EXP):
+        result = zout[0, q].astype(jnp.float32)
+        for j in (1, 2, 3):
+            result = result + zout[j, q].astype(jnp.float32)
+        out_ref[q * share : (q + 1) * share, :] = result.astype(jnp.bfloat16)
+
+    for d in (1, 2, 3):
+        head_copy(d).wait_send()
+        z_copy(d).wait_send()
+    for d in range(PLANE_EXP):
+        for pos in range(4):
+            mate_copy(pos, d).wait_send()
+            core_copy(pos, d).wait_send()
+        for pos in (1, 2):
+            near_copy(pos, d).wait_send()
+            far_copy(pos, d).wait_send()
+            first_copy(pos, d).wait_send()
+            corner_copy(pos, d).wait_send()
+            second_copy(pos, d).wait_send()
+        for j in (1, 2, 3):
+            out_copy(d, j).wait_send()
+
+
+def plane_layer(attended, hidden_in, gain, gate_rows, out_proj, gate_up, down_proj):
+    blk, width = hidden_in.shape
+    units = gate_up.shape[-1]
+    share, col = blk // PLANE_EXP, width // PLANE_EXP
+    kind = jnp.bfloat16
+    copies = 96
+    return pl.pallas_call(
+        layer_kernel,
+        out_shape=jax.ShapeDtypeStruct((blk, col), kind),
+        in_specs=[pl.BlockSpec(memory_space=pltpu.VMEM)] * 4
+        + [pl.BlockSpec(memory_space=pl.ANY)] * 3,
+        out_specs=pl.BlockSpec(memory_space=pltpu.VMEM),
+        scratch_shapes=[
+            pltpu.VMEM((width, out_proj.shape[0]), kind),
+            pltpu.VMEM((2, units, width), kind),
+            pltpu.VMEM((units, width), kind),
+            pltpu.VMEM((blk, width), kind),
+            pltpu.VMEM((blk, width), jnp.float32),
+            pltpu.VMEM((PLANE_EXP, share, width), kind),
+            pltpu.VMEM((share, width), jnp.float32),
+            pltpu.VMEM((PLANE_EXP, PLANE_CTX, share, width), kind),
+            pltpu.VMEM((PLANE_EXP, PLANE_CTX, share, width), kind),
+            pltpu.VMEM((PLANE_EXP, 4, share, width), kind),
+            pltpu.VMEM((PLANE_EXP, 2, share // 2, width), kind),
+            pltpu.VMEM((PLANE_EXP, 2, share // 2, width), kind),
+            pltpu.VMEM((PLANE_EXP, 2, share // 2, width), kind),
+            pltpu.VMEM((share, width), jnp.float32),
+            pltpu.VMEM((PLANE_EXP, PLANE_EXP, share, col), kind),
+            pltpu.VMEM((PLANE_EXP, PLANE_EXP, share, col), kind),
+            pltpu.SemaphoreType.DMA((copies,)),
+            pltpu.SemaphoreType.DMA((copies,)),
+            pltpu.SemaphoreType.DMA((3,)),
+        ],
+        compiler_params=pltpu.CompilerParams(
+            collective_id=0, has_side_effects=True, vmem_limit_bytes=58 * 1024 * 1024
+        ),
+    )(
+        attended,
+        hidden_in.T,
+        gain.reshape(1, width),
+        gate_rows,
+        out_proj.T,
+        gate_up[0].transpose(1, 2, 0),
+        down_proj[0],
+    )
+
+
+def gather_kernel(mine_ref, all_ref, send_sems, recv_sems, own_sem):
+    c, e = lax.axis_index("ctx"), lax.axis_index("exp")
+    count = all_ref.shape[0]
+    own = pltpu.make_async_copy(mine_ref, all_ref.at[c], own_sem)
+    own.start()
+    barrier = pltpu.get_barrier_semaphore()
+    for d in range(1, count):
+        pl.semaphore_signal(
+            barrier,
+            inc=1,
+            device_id=((c + d) % count, e),
+            device_id_type=pl.DeviceIdType.MESH,
+        )
+    pl.semaphore_wait(barrier, count - 1)
+    copies = [
+        pltpu.make_async_remote_copy(
+            src_ref=mine_ref,
+            dst_ref=all_ref.at[c],
+            send_sem=send_sems.at[d],
+            recv_sem=recv_sems.at[d],
+            device_id=((c + d) % count, e),
+            device_id_type=pl.DeviceIdType.MESH,
+        )
+        for d in range(1, count)
+    ]
+    for item in copies:
+        item.start()
+    own.wait()
+    for item in copies:
+        item.wait()
+
+
+def plane_gather(mine):
+    return pl.pallas_call(
+        gather_kernel,
+        out_shape=jax.ShapeDtypeStruct((PLANE_CTX, *mine.shape), mine.dtype),
+        in_specs=[pl.BlockSpec(memory_space=pltpu.VMEM)],
+        out_specs=pl.BlockSpec(memory_space=pltpu.VMEM),
+        scratch_shapes=[
+            pltpu.SemaphoreType.DMA((PLANE_CTX,)),
+            pltpu.SemaphoreType.DMA((PLANE_CTX,)),
+            pltpu.SemaphoreType.DMA,
+        ],
+        compiler_params=pltpu.CompilerParams(
+            collective_id=1, has_side_effects=True, vmem_limit_bytes=8 * 1024 * 1024
+        ),
+    )(mine)
 
 
 def per_device(
@@ -104,12 +449,31 @@
     gate_high = expert_gates.astype(jnp.bfloat16)
     gate_low = (expert_gates - gate_high.astype(jnp.float32)).astype(jnp.bfloat16)
     top_count = expert_ids.shape[1]
-    key_value = jnp.concatenate([key_rot, value_block, ids_part, gate_high, gate_low], axis=1)
     score_scale = 1.0 / math.sqrt(HEAD_SIZE)
-    block_part = lax.all_gather(key_value, "ctx", axis=0, tiled=True)
-    routing = block_part[:, 2 * HEAD_SIZE :].astype(jnp.float32)
-    all_ids = routing[:, :top_count]
-    all_gates = routing[:, top_count : 2 * top_count] + routing[:, 2 * top_count :]
+    in_plane = ctx_count == PLANE_CTX and exp_count == PLANE_EXP
+    if in_plane:
+        key_value = jnp.concatenate([key_rot, value_block], axis=1)
+        routing = jnp.concatenate([ids_part, gate_high, gate_low], axis=1).T
+        routing = jnp.pad(routing, ((0, -routing.shape[0] % 16), (0, 0)))
+        gathered = plane_gather(jnp.concatenate([key_value, routing], axis=0))
+        block_part = gathered[:, :tok_rows].reshape(ctx_count * tok_rows, 2 * HEAD_SIZE)
+        routing = gathered[:, tok_rows:].astype(jnp.float32)
+        both = (
+            routing[:, top_count : 2 * top_count] + routing[:, 2 * top_count : 3 * top_count]
+        )
+        mine = routing[:, :top_count] == lax.axis_index("ctx").astype(jnp.float32)
+        gate_rows = (
+            jnp.sum(jnp.where(mine, both, 0.0), axis=1)
+            .reshape(ctx_count, exp_count, tok_rows // exp_count)
+            .transpose(1, 0, 2)
+            .reshape(exp_count, 1, ctx_count * tok_rows // exp_count)
+        )
+    else:
+        key_value = jnp.concatenate([key_rot, value_block, ids_part, gate_high, gate_low], axis=1)
+        block_part = lax.all_gather(key_value, "ctx", axis=0, tiled=True)
+        routing = block_part[:, 2 * HEAD_SIZE :].astype(jnp.float32)
+        all_ids = routing[:, :top_count]
+        all_gates = routing[:, top_count : 2 * top_count] + routing[:, 2 * top_count :]
     run_max = jnp.broadcast_to(sink_logits[:, None], (local_heads, tok_rows))
     run_total = jnp.ones((local_heads, tok_rows), jnp.float32)
     run_sum = jnp.zeros((local_heads, tok_rows, HEAD_SIZE), jnp.float32)
@@ -136,20 +500,23 @@
         .reshape(tok_rows, local_heads * HEAD_SIZE)
         .astype(jnp.bfloat16)
     )
-    head_part = jnp.dot(attended, out_proj, preferred_element_type=jnp.float32)
+    if in_plane:
+        return plane_layer(
+            attended, hidden_in, norm_gain, gate_rows, out_proj, gate_up, down_proj
+        )
     share_rows = tok_rows // exp_count
     my_row = lax.axis_index("exp") * share_rows
-    residual = lax.dynamic_slice_in_dim(hidden_in, my_row, share_rows, 0).astype(
-        jnp.float32
-    ) + lax.psum_scatter(
+    n_experts = gate_up.shape[0] * ctx_count
+    capacity = max(2, tok_rows * top_count * 5 // (4 * n_experts))
+    pick, weighted = routing_matrices(all_ids, all_gates, ctx_count, tok_rows, capacity)
+    head_part = jnp.dot(attended, out_proj, preferred_element_type=jnp.float32)
+    hidden_share = lax.dynamic_slice_in_dim(hidden_in, my_row, share_rows, 0)
+    residual = hidden_share.astype(jnp.float32) + lax.psum_scatter(
         head_part.astype(jnp.bfloat16), "exp", scatter_dimension=0, tiled=True
     ).astype(jnp.float32)
     mean_square = jnp.mean(residual * residual, axis=1, keepdims=True)
     normed = (residual * lax.rsqrt(mean_square + 1e-05) * norm_gain[None, :]).astype(jnp.bfloat16)
     all_normed = lax.all_gather(normed, ("ctx", "exp"), axis=0, tiled=True)
-    n_experts = gate_up.shape[0] * ctx_count
-    capacity = max(2, tok_rows * top_count * 5 // (4 * n_experts))
-    pick, weighted = routing_matrices(all_ids, all_gates, ctx_count, tok_rows, capacity)
     expert_rows = jnp.einsum(
         "bst,btd->bsd",
         pick,

time: 261 us -> 123 us (0.47)
  waiting for transfers between devices: 169 us -> 0 us
  Pallas kernels: 0 us -> 108 us
  matrix products: 32.7 us -> 3.2 us
  local copies, waits for them, and re-layouts: 22.7 us -> 5.69 us
  between operations: 13.4 us -> 0.11 us
  blocking collectives: 12 us -> 0 us
  other arithmetic: 10.3 us -> 5.47 us
    pallas_call x0 -> x2, Pallas kernels: none -> 108 us  [the longest x1 99.4 us: plane_layer(): pl.pallas_call(layer_kernel, out_shape=jax.ShapeDtypeStruct((blk, col), k...]
    reduce_scatter x2 -> x0, waiting for transfers between devices: 79.1 us -> none  [the longest x1 59.4 us: per_device(): lax.psum_scatter(spread.reshape(ctx_count * tok_rows, D), 'ctx', scatter_...]
    all_gather x1 -> x0, waiting for transfers between devices: 66.3 us -> none  [per_device(): all_normed = lax.all_gather(normed, ('ctx', 'exp'), axis=0, tiled=True)]
    dot_general x6 -> x0, matrix products: 27.8 us -> none  [the longest x1 9.47 us: per_device(): jnp.dot(expert_rows, gate_up.reshape(D, 2 * unit_count), preferred_elemen...]
    unnamed x5 -> x0, waiting for transfers between devices: 23.1 us -> none
    convert_element_type x2 -> x1, local copies, waits for them, and re-layouts: 14.6 us -> 0.77 us  [per_device(): attended = (run_sum / run_total[:, :, None]).transpose(1, 0, 2).reshape(t...]
    all_gather x1 -> x0, blocking collectives: 12 us -> none  [per_device(): block_part = lax.all_gather(key_value, 'ctx', axis=0, tiled=True)]
    convert_element_type x5 -> x1, other arithmetic: 4.67 us -> 0.01 us  [per_device(): routing = gathered[:, tok_rows:].astype(jnp.float32)]
  transfers between devices with their start and end apart: 4 -> 0, of which waited for: 4 -> 0; matrix products, arithmetic and copies ran while one was open for 2% -> 0% of each run, Pallas kernels for 0% -> 0%
where the time goes in v4:
time: 123 us; the launch traced here: 122 us
  Pallas kernels  108 us (88%)
  local copies, waits for them, and re-layouts  5.69 us (5%)
  other arithmetic  5.47 us (4%)
  matrix products  3.2 us (3%)
    pallas_call x1, Pallas kernels, plane_layer(): pl.pallas_call(layer_kernel, out_shape=jax.ShapeDtypeStruct((blk, col), k...  99.4 us
    pallas_call x1, Pallas kernels, plane_gather(): pl.pallas_call(gather_kernel, out_shape=jax.ShapeDtypeStruct((PLANE_CTX,...  8.55 us
    dot_general x1, matrix products, per_device(): jnp.einsum('hrk,kd->hrd', weights, value_part, precision=lax.Precision.HI...  2.51 us

profile of v4, /device:TPU:0, one launch (start us, length us, event | category | flops | bytes accessed | tf_op | source)
XLA Modules:
  0.0 122.4 jit_solution(2553256743385622552)
XLA Ops:
  0.0 0.0 copy-start
  0.0 0.0 copy-start.1
  0.0 0.7 convert_element_type.43
  0.7 0.8 subtract_convert_fusion.1
  1.5 1.3 %reshape.270.gain_ref = f32[1,2880]{1,0:T(1,128)} reshape(f32[2880]{0:T(1024)} %param.19) | data formatting | bytes 23040 | tf_op jit(solution)/shard_map/reshape | solution.py:358
  2.8 0.0 copy-done
  2.8 0.1 constant_dynamic-slice_fusion
  2.9 0.8 fusion.27
  3.7 0.8 bitcast_convert_fusion
  4.5 1.0 fusion.20
  5.5 0.1 maximum_bitcast_fusion
  5.6 0.1 fusion.26.mine_ref
  5.7 0.1 iota_compare_fusion
  5.8 8.5 %shard_map.127 = bf16[8,144,128]{2,1,0:T(8,128)(2,1)S(1)} custom-call(bf16[144,128]{1,0:T(8,128)(2,1)S(1)} %fusion.26.mine_ref), custom_call_target="tpu_custom_call" | custom-call | tf_op jit(solution)/shard_map/pallas_call | solution.py:399
  14.4 0.1 reshape.271
  14.5 0.7 reshape.272.gate_ref
  15.2 1.0 copy.29
  16.2 0.7 fusion.2
  16.9 0.0 copy-done.1
  17.0 0.1 broadcast_maximum_fusion
  17.0 0.9 fusion
  17.9 0.1 multiply_bitcast_fusion
  18.0 2.5 %fusion.10 = bf16[128,8,64]{0,2,1:T(8,128)(2,1)S(1)} fusion(f32[1024,128,8]{1,0,2:T(8,128)S(1)} %get-tuple-element.16, f32[8,128]{1,0:T(8,128)S(1)} %broadcast_maximum_fusion, pred[128,1024]{0,1:T(8,128)(4,1)S(1)} %iota_compare_fusion, bf16[1024,128]{1,0:T(8,128)(2,1)S(1)} %bitcast.61, f32[128,8]{0,1:T(8,128)S(1)} %get-tuple-element.12, ...), kind=kOutput, calls=%fused_computation.12 | convolution fusion | flops 808648704 | bytes 4730880 | tf_op jit(solution)/shard_map/hrk,kd->hrd/dot_general | solution.py:493
  20.5 0.8 copy.33.attended_ref
  21.3 99.4 %shard_map.128 = bf16[128,720]{1,0:T(8,128)(2,1)} custom-call(bf16[128,512]{1,0:T(8,128)(2,1)} %copy.33.attended_ref, bf16[2880,128]{1,0:T(8,128)(2,1)} %bitcast.62, f32[1,2880]{1,0:T(1,128)} %reshape.270.gain_ref, f32[4,1,256]{2,1,0:T(1,128)} %reshape.272.gate_ref, bf16[2880,512]{1,0:T(8,128)(2,1)} %bitcast.58, bf16[2,720,2880]{2,1,0:T(8,128)(2,1)} %bitcast.56, ...), custom_call_target="tpu_custom_call" | custom-call | tf_op jit(solution)/shard_map/pallas_call | solution.py:325
  120.7 1.7 %copy.34 = bf16[128,720]{0,1:T(8,128)(2,1)} copy(bf16[128,720]{1,0:T(8,128)(2,1)} %shard_map.128) | data formatting | bytes 368640 | tf_op jit(solution)/shard_map/pallas_call | solution.py:325
  (7 shorter events, 0.1 us)
Async XLA Ops:
  0.0 2.8 %copy-start = (bf16[128,256]{1,0:T(8,128)(2,1)S(1)}, bf16[128,256]{1,0:T(8,128)(2,1)}, u32[]{:S(2)}) copy-start(bf16[128,256]{1,0:T(8,128)(2,1)} %param.16) | copy-start | bytes 196612
  0.0 16.9 %copy-start.1 = (f32[8]{0:T(128)S(1)}, f32[8]{0:T(128)}, u32[]{:S(2)}) copy-start(f32[8]{0:T(128)} %param.17) | copy-start | bytes 100

commit v5 on v4

--- a/solution.py
+++ b/solution.py
@@ -240,34 +240,37 @@
         for j in (2, 1, 3):
             out_copy(d, j).start()
 
-    for d in (2, 1, 3):
-        z_copy(d).start()
-    spread_near(0)
-
-    def before(d):
-        spread_far(d)
-        if d + 1 < PLANE_EXP:
-            z_copy(d + 1).wait_recv()
-            spread_near(d + 1)
-        finish_spread(d)
-        if d == 0:
+    order = (0, 1, 3, 2)
+    z_copy(order[1]).start()
+    spread_near(order[0])
+
+    def before(i):
+        spread_far(order[i])
+        if i == 0:
+            z_copy(order[2]).start()
+        if i + 1 < PLANE_EXP:
+            z_copy(order[i + 1]).wait_recv()
+            spread_near(order[i + 1])
+        finish_spread(order[i])
+        if i == 0:
+            z_copy(order[3]).start()
             load_gu.wait()
             load_down.wait()
-        if d >= 1:
-            sum_cores(d - 1)
-        if d >= 2:
-            finish_sum(d - 2)
-
-    def after(d):
+        if i >= 1:
+            sum_cores(order[i - 1])
+        if i >= 2:
+            finish_sum(order[i - 2])
+
+    def after(i):
         for pos in (3, 1, 2, 0):
-            core_copy(pos, d).start()
-        if d >= 1:
-            sum_corners(d - 1)
-
-    def step(d, carry):
+            core_copy(pos, order[i]).start()
+        if i >= 1:
+            sum_corners(order[i - 1])
+
+    def step(i, carry):
         for now in range(PLANE_EXP):
-            pl.when(d == now)(functools.partial(before, now))
-        part = quarter(d)
+            pl.when(i == now)(functools.partial(before, now))
+        part = quarter(i + i // 2 * (5 - 2 * i))
         tokens = normed[part].reshape(-1, width)
         gate = lax.dot_general(gu[0], tokens, across, preferred_element_type=jnp.float32)
         up = lax.dot_general(gu[1], tokens, across, preferred_element_type=jnp.float32)
@@ -280,15 +283,14 @@
             .reshape(-1, share, width)
         )
         for now in range(PLANE_EXP):
-            pl.when(d == now)(functools.partial(after, now))
+            pl.when(i == now)(functools.partial(after, now))
         return carry
 
     lax.fori_loop(0, PLANE_EXP, step, 0)
-    last = PLANE_EXP - 1
-    sum_cores(last)
-    finish_sum(last - 1)
-    sum_corners(last)
-    finish_sum(last)
+    sum_cores(order[3])
+    finish_sum(order[2])
+    sum_corners(order[3])
+    finish_sum(order[3])
     for d in range(PLANE_EXP):
         zout[0, quarter(d)] = stage[d, e]
         for j in (1, 2, 3):

time: 123 us -> 119 us (0.967)
  Pallas kernels: 108 us -> 104 us
    pallas_call x1, Pallas kernels: 99.4 us -> 95.5 us  [plane_layer(): pl.pallas_call(layer_kernel, out_shape=jax.ShapeDtypeStruct((blk, col), k...]
where the time goes in v5:
time: 119 us; the launch traced here: 118 us
  Pallas kernels  104 us (87%)
  local copies, waits for them, and re-layouts  5.69 us (5%)
  other arithmetic  5.47 us (5%)
  matrix products  3.2 us (3%)
    pallas_call x1, Pallas kernels, plane_layer(): pl.pallas_call(layer_kernel, out_shape=jax.ShapeDtypeStruct((blk, col), k...  95.5 us
    pallas_call x1, Pallas kernels, plane_gather(): pl.pallas_call(gather_kernel, out_shape=jax.ShapeDtypeStruct((PLANE_CTX,...  8.55 us
    dot_general x1, matrix products, per_device(): jnp.einsum('hrk,kd->hrd', weights, value_part, precision=lax.Precision.HI...  2.51 us

profile of v5, /device:TPU:0, one launch (start us, length us, event | category | flops | bytes accessed | tf_op | source)
XLA Modules:
  0.0 118.5 jit_solution(2080986607684975377)
XLA Ops:
  0.0 0.0 copy-start
  0.0 0.0 copy-start.1
  0.0 0.7 convert_element_type.43
  0.7 0.8 subtract_convert_fusion.1
  1.5 1.3 %reshape.270.gain_ref = f32[1,2880]{1,0:T(1,128)} reshape(f32[2880]{0:T(1024)} %param.19) | data formatting | bytes 23040 | tf_op jit(solution)/shard_map/reshape | solution.py:360
  2.8 0.0 copy-done
  2.8 0.1 constant_dynamic-slice_fusion
  2.9 0.8 fusion.27
  3.7 0.8 bitcast_convert_fusion
  4.5 1.0 fusion.20
  5.5 0.1 maximum_bitcast_fusion
  5.6 0.1 fusion.26.mine_ref
  5.7 0.1 iota_compare_fusion
  5.8 8.5 %shard_map.127 = bf16[8,144,128]{2,1,0:T(8,128)(2,1)S(1)} custom-call(bf16[144,128]{1,0:T(8,128)(2,1)S(1)} %fusion.26.mine_ref), custom_call_target="tpu_custom_call" | custom-call | tf_op jit(solution)/shard_map/pallas_call | solution.py:401
  14.4 0.1 reshape.271
  14.5 0.7 reshape.272.gate_ref
  15.2 1.0 copy.29
  16.2 0.7 fusion.2
  16.9 0.0 copy-done.1
  17.0 0.1 broadcast_maximum_fusion
  17.0 0.9 fusion
  17.9 0.1 multiply_bitcast_fusion
  18.0 2.5 %fusion.10 = bf16[128,8,64]{0,2,1:T(8,128)(2,1)S(1)} fusion(f32[1024,128,8]{1,0,2:T(8,128)S(1)} %get-tuple-element.16, f32[8,128]{1,0:T(8,128)S(1)} %broadcast_maximum_fusion, pred[128,1024]{0,1:T(8,128)(4,1)S(1)} %iota_compare_fusion, bf16[1024,128]{1,0:T(8,128)(2,1)S(1)} %bitcast.61, f32[128,8]{0,1:T(8,128)S(1)} %get-tuple-element.12, ...), kind=kOutput, calls=%fused_computation.12 | convolution fusion | flops 808648704 | bytes 4730880 | tf_op jit(solution)/shard_map/hrk,kd->hrd/dot_general | solution.py:495
  20.5 0.8 copy.33.attended_ref
  21.3 95.5 %shard_map.128 = bf16[128,720]{1,0:T(8,128)(2,1)} custom-call(bf16[128,512]{1,0:T(8,128)(2,1)} %copy.33.attended_ref, bf16[2880,128]{1,0:T(8,128)(2,1)} %bitcast.62, f32[1,2880]{1,0:T(1,128)} %reshape.270.gain_ref, f32[4,1,256]{2,1,0:T(1,128)} %reshape.272.gate_ref, bf16[2880,512]{1,0:T(8,128)(2,1)} %bitcast.58, bf16[2,720,2880]{2,1,0:T(8,128)(2,1)} %bitcast.56, ...), custom_call_target="tpu_custom_call" | custom-call | tf_op jit(solution)/shard_map/pallas_call | solution.py:327
  116.8 1.7 %copy.34 = bf16[128,720]{0,1:T(8,128)(2,1)} copy(bf16[128,720]{1,0:T(8,128)(2,1)} %shard_map.128) | data formatting | bytes 368640 | tf_op jit(solution)/shard_map/pallas_call | solution.py:327
  (7 shorter events, 0.1 us)
Async XLA Ops:
  0.0 2.8 %copy-start = (bf16[128,256]{1,0:T(8,128)(2,1)S(1)}, bf16[128,256]{1,0:T(8,128)(2,1)}, u32[]{:S(2)}) copy-start(bf16[128,256]{1,0:T(8,128)(2,1)} %param.16) | copy-start | bytes 196612
  0.0 16.9 %copy-start.1 = (f32[8]{0:T(128)S(1)}, f32[8]{0:T(128)}, u32[]{:S(2)}) copy-start(f32[8]{0:T(128)} %param.17) | copy-start | bytes 100
